TPU v7x, 512 devices: a whole 4x4x16 slice. The times are simulated.
512 devices in a mesh: ctx: 128 (over z, x, core), tp: 4 (over y).
Axes of the slice: x: 4, y: 4, z: 16, core: 2. Of those that a mesh axis runs over, the one named last changes fastest.
Arguments:
- queries: bfloat16 [32768, 2048], P('ctx', 'tp'), may hold values from -8 to 8
- key_proj: bfloat16 [32768, 2048], P('ctx', 'tp'), may hold values from -8 to 8
- value_proj: bfloat16 [32768, 2048], P('ctx', 'tp'), may hold values from -4 to 4
- router: bfloat16 [32768], P('ctx'), may hold values from 0.5 to 2
- chosen: int32 [16, 256], replicated, may hold values from 0 to 32767, as said below
- out_weight: bfloat16 [2048, 4096], P('tp'), may hold values from -0.125 to 0.125
Outputs:
- update: bfloat16 [32768, 4096], P('ctx', 'tp')
Inputs may be any that keep to these rules, and one draw needn't show every extreme that they name: `chosen`: row b holds 256 ascending positions of b * 2048 to b * 2048 + 2047. Each run of 128 positions that starts at a multiple of 128 holds at most 32 of them, and in every row one such run holds exactly 32.
All inputs are finite; a program needn't handle non-finite values.
Results may differ from a plain program's by a relative error of at most 0.017.
Values may be sent and summed in bfloat16 or wider, within the bound.
A program may use at most 128 MiB of HBM per device.

v0:
```python
import jax
import jax.numpy as jnp
from jax import lax
from jax.sharding import PartitionSpec as P

HD = 128


NEG_FILL = -1e30


def attend(query_rows, query_pos, pair_rows, key_pos):
    row_count = query_rows.shape[0]
    head_count = query_rows.shape[1] // HD
    shaped = query_rows.reshape(row_count, head_count, HD)
    factor_scale = HD ** (-0.5)
    top_now = jnp.full((head_count, row_count), NEG_FILL, jnp.float32)
    pair_part = lax.all_gather(pair_rows, "ctx", axis=0, tiled=True)
    pos_part = lax.all_gather(key_pos, "ctx", axis=0, tiled=True)
    part_rows = pair_part.shape[0]
    key_part = pair_part[:, 0].reshape(part_rows, head_count, HD)
    value_part = pair_part[:, 1].reshape(part_rows, head_count, HD)
    scores = (
        jnp.einsum("qhd,khd->hqk", shaped, key_part, preferred_element_type=jnp.float32)
        * factor_scale
    )
    allowed = pos_part[None, None, :] <= query_pos[None, :, None]
    masked = jnp.where(allowed, scores, NEG_FILL)
    top_new = jnp.maximum(top_now, jnp.max(masked, axis=2))
    weights = jnp.where(allowed, jnp.exp(masked - top_new[:, :, None]), 0.0)
    total_new = jnp.sum(weights, axis=2)
    added = jnp.einsum(
        "hqk,khd->hqd", weights.astype(jnp.bfloat16), value_part, preferred_element_type=jnp.float32
    )
    attended = added / total_new[:, :, None]
    return (
        jnp.transpose(attended, (1, 0, 2)).reshape(row_count, head_count * HD).astype(jnp.bfloat16)
    )


def project(attended, out_weight):
    return (
        lax.psum_scatter(
            lax.dot_general(
                out_weight, attended, (((0,), (1,)), ((), ())), preferred_element_type=jnp.float32
            ).astype(jnp.bfloat16),
            "tp",
            scatter_dimension=0,
            tiled=True,
        )
        .astype(jnp.float32)
        .T
    )


def shards(queries, key_proj, value_proj, router, chosen, out_weight):
    tok_rows = queries.shape[0]
    piece_len = tok_rows // 2
    piece_most = piece_len // 4
    devices = lax.axis_size("ctx")
    device = lax.axis_index("ctx")
    block_len = 8 * chosen.shape[1]
    seq_len = 2 * devices * piece_len
    padded = jnp.concatenate(
        [chosen, jnp.full((chosen.shape[0], piece_most), seq_len, jnp.int32)], axis=1
    )
    pos_parts = []
    row_parts = []
    live_parts = []
    count_parts = []
    for half_index in range(2):
        piece_id = device if half_index == 0 else 2 * devices - 1 - device
        entries = lax.dynamic_index_in_dim(
            padded, piece_id * piece_len // block_len, 0, keepdims=False
        )
        entry_piece = entries // piece_len
        start_at = jnp.sum((entry_piece < piece_id).astype(jnp.int32))
        live_count = jnp.sum((entry_piece == piece_id).astype(jnp.int32))
        window = lax.dynamic_slice_in_dim(entries, start_at, piece_most)
        live_mask = jnp.arange(piece_most) < live_count
        pos_parts.append(jnp.where(live_mask, window, seq_len))
        row_parts.append(
            jnp.where(live_mask, window - piece_id * piece_len + half_index * piece_len, 0)
        )
        live_parts.append(live_mask)
        count_parts.append(live_count)
    positions = jnp.concatenate(pos_parts)
    local_rows = jnp.concatenate(row_parts)
    live_all = jnp.concatenate(live_parts)
    query_rows = jnp.take(queries, local_rows, axis=0)
    key_rows = jnp.take(key_proj, local_rows, axis=0)
    value_rows = jnp.take(value_proj, local_rows, axis=0)
    router_rows = jnp.take(router, local_rows, axis=0)
    attended = attend(query_rows, positions, jnp.stack([key_rows, value_rows], axis=1), positions)
    projected = project(attended, out_weight)
    updates = (projected * router_rows.astype(jnp.float32)[:, None]).astype(jnp.bfloat16)
    placer = ((local_rows[None, :] == jnp.arange(tok_rows)[:, None]) & live_all[None, :]).astype(
        jnp.bfloat16
    )
    return jnp.dot(placer, updates, preferred_element_type=jnp.float32).astype(jnp.bfloat16)


def solution(mesh):
    placed = (P("ctx", "tp"), P("ctx", "tp"), P("ctx", "tp"), P("ctx"), P(), P("tp", None))
    return jax.shard_map(
        shards, mesh=mesh, in_specs=placed, out_specs=P("ctx", "tp"), check_vma=False
    )
```

profile of v0, /device:TPU:1, one launch (start us, length us, event | category | flops | bytes accessed | tf_op | source)
XLA Modules:
  0.0 619.6 jit_solution(4837082991886154404)
XLA Ops:
  6.5 0.8 fusion.34
  7.3 0.7 convert_reduce_fusion.1
  9.4 0.7 convert_reduce_fusion.3
  12.8 2.1 bitcast_select_fusion.1
  14.8 1.3 fusion.38
  16.1 0.1 fusion.36
  16.2 1.4 gather_fusion
  17.7 0.1 select_convert_fusion
  17.8 0.7 gather_fusion.1
  18.5 1.7 gather_fusion.2
  20.2 1.7 gather_fusion.3
  21.9 0.1 select_bitcast_fusion.2
  22.0 0.7 pad_maximum_fusion
  22.6 0.0 all-gather.2.cloned.1.call-update
  22.7 0.0 reduce-scatter.2.cloned.1.call-start
  22.7 1.3 dynamic-slice.2
  24.6 0.2 fusion.41
  24.8 498.9 %all-reduce.1 = s32[8192]{0:T(1024)S(1)} all-reduce(s32[8192]{0:T(1024)S(1)} %get-tuple-element.15), channel_id=1, replica_groups=mesh['ctx'=128,'tp'=4] {'ctx'}, use_global_device_ids=true, to_apply=%add.1 | all-reduce | flops 8192 | bytes 65536
  523.6 0.3 broadcast_compare_fusion
  524.0 0.0 all-gather.2.cloned.1.call-done
  524.0 11.3 %fusion.42 = (bf16[8192,1,512]{2,0,1:T(8,128)(2,1)}, bf16[8192,1,512]{2,0,1:T(8,128)(2,1)}) fusion(bf16[8192,2,512]{2,0,1:T(8,128)(2,1)} %all-gather.2.cloned.1.call-done), kind=kLoop, calls=%fused_computation.81 | loop fusion | bytes 33554432 | tf_op jit(solution)/shard_map/slice | solution.py:21
  535.3 11.4 %copy.8 = bf16[8192,1,512]{0,2,1:T(8,128)(2,1)} copy(bf16[8192,1,512]{2,0,1:T(8,128)(2,1)} %get-tuple-element.21) | data formatting | bytes 16777216 | tf_op jit(solution)/shard_map/slice | solution.py:21
  546.7 9.3 %fusion.43 = (f32[4,64]{1,0:T(4,128)S(1)}, f32[4,64,8192]{2,1,0:T(8,128)}) fusion(bf16[8192,4,128]{0,2,1:T(8,128)(2,1)} %bitcast.49, bf16[8,4,8,128]{3,2,1,0:T(8,128)(2,1)S(1)} %get-tuple-element.25, pred[64,8192]{1,0:T(8,128)(4,1)S(1)} %broadcast_compare_fusion), kind=kOutput, calls=%fused_computation.82 | convolution fusion | flops 543162112 | bytes 17368064 | tf_op jit(solution)/shard_map/qhd,khd->hqk/dot_general | solution.py:24
  556.0 11.4 %copy.11 = bf16[8192,1,512]{0,2,1:T(8,128)(2,1)} copy(bf16[8192,1,512]{2,0,1:T(8,128)(2,1)} %get-tuple-element.22) | data formatting | bytes 16777216 | tf_op jit(solution)/shard_map/slice | solution.py:22
  567.3 5.3 fusion.1
  572.7 8.9 %fusion.18 = bf16[4,8,8,128]{3,2,1,0:T(8,128)(2,1)S(1)} fusion(bf16[8192,4,128]{0,2,1:T(8,128)(2,1)} %bitcast.50, f32[4,64,8192]{2,1,0:T(8,128)} %get-tuple-element.29, f32[4,64]{1,0:T(4,128)S(1)} %broadcast_maximum_fusion, pred[64,8192]{1,0:T(8,128)(4,1)S(1)} %broadcast_compare_fusion, f32[64,4]{0,1:T(4,128)S(1)} %bitcast.53), kind=kOutput, calls=%fused_computation.19 | convolution fusion | flops 543227904 | bytes 17369088 | tf_op jit(solution)/shard_map/hqk,khd->hqd/dot_general | solution.py:32
  581.6 3.8 fusion.3
  585.4 0.0 reduce-scatter.2.cloned.1.call-update
  585.4 1.3 iota_compare_fusion.1
  586.7 0.1 pad_add_fusion
  586.8 23.9 %reduce-scatter.2.cloned.1.call-done = bf16[1024,64]{0,1:T(8,128)(2,1)} async-done(((bf16[4096,64]{0,1:T(8,128)(2,1)}), bf16[1024,64]{0,1:T(8,128)(2,1)}) %reduce-scatter.2.cloned.1.call-update) | async-done | bytes 131088 | tf_op jit(solution)/shard_map/reduce_scatter | solution.py:43
  610.7 2.1 convolution_convert_fusion.1
  (8 shorter events, 0.0 us)
Async XLA Ops:
  6.5 11.2 %copy-start = (bf16[256,512]{1,0:T(8,128)(2,1)S(1)}, bf16[256,512]{1,0:T(8,128)(2,1)}, u32[]{:S(2)}) copy-start(bf16[256,512]{1,0:T(8,128)(2,1)} %param.8) | copy-start | bytes 786436
  6.5 517.5 %all-gather.2.cloned.1.call-start = ((), (), s32[]{:S(2)}) async-start(), calls=%async_computation.1 | async-start | bytes 16908288 | tf_op jit(solution)/shard_map/all_gather | solution.py:18
  22.7 588.0 %reduce-scatter.2.cloned.1.call-start = ((), (), s32[]{:S(2)}) async-start(), calls=%async_computation.2 | async-start | bytes 655360 | tf_op jit(solution)/shard_map/reduce_scatter | solution.py:43
Sparse Core Ops, SparseCore 0:
  22.8 164.4 all-gather.1
  585.5 25.1 reduce-scatter.1
where the time goes:
time: 621 us; the launch traced here: 620 us
  blocking collectives  499 us (80%)
  local copies, waits for them, and re-layouts  41.6 us (7%)
  matrix products  24.1 us (4%)
  waiting for transfers between devices  24 us (4%)
  between operations  18.1 us (3%)
  other arithmetic  13 us (2%)
    unnamed x1, blocking collectives  499 us
    reduce_scatter x1, waiting for transfers between devices, project(): lax.psum_scatter(lax.dot_general(out_weight, attended, (((0,), (1,)), (()...  23.9 us
    slice x2, local copies, waits for them, and re-layouts, attend(): key_part = pair_part[:, 0].reshape(part_rows, head_count, HD)  22.7 us
  transfers between devices with their start and end apart: 2, of which 1 were waited for; matrix products, arithmetic and copies ran while one was open for 1% of the time, Pallas kernels for 0%

commit v1 on v0

v1 whole, which is shorter than its diff:
```python
import functools
import jax
import jax.numpy as jnp
from jax import lax
from jax.experimental import pallas as pl
from jax.experimental.pallas import tpu as pltpu
from jax.sharding import PartitionSpec as P

HD = 128
PIECE = 128
MOST = 32
PICK = 256
GROUP = 16
CHIPS = 8
RING = 16
SUBS = 4
SUB = PICK // SUBS
MESH = pl.DeviceIdType.MESH
F32 = jnp.float32
BF16 = jnp.bfloat16


def one_hots(chosen_row, base):
    first = jnp.sum((chosen_row < base).astype(jnp.int32), axis=1, keepdims=True)
    inside = (chosen_row >= base) & (chosen_row < base + PIECE)
    entry = lax.broadcasted_iota(jnp.int32, (MOST, PICK), 1)
    rank = lax.broadcasted_iota(jnp.int32, (MOST, PICK), 0)
    by_rank = (entry - first == rank) & inside
    token = lax.broadcasted_iota(jnp.int32, (PIECE, PICK), 0)
    by_token = chosen_row - base == token
    return by_rank.astype(F32).astype(BF16), by_token.astype(F32).astype(BF16)


def dot_nt(a, b):
    return lax.dot_general(a, b, (((1,), (1,)), ((), ())), preferred_element_type=F32)


def body(
    q_ref, k_ref, v_ref, router_ref, chosen_ref, w_hbm, out_ref,
    sel, kvpad, qpad, kv, att, osend, wbuf, place, rsel, top, total, acc, pick,
    s1, r1_kv, r1_q, s2, r2_right, r2_left, s_sib, r_sib, s3, r3, s_w, r_w, s_wf, r_wf, l_w,
):
    ctx = lax.axis_index("ctx")
    y = lax.axis_index("tp")
    z = ctx // 8
    core = ctx % 2
    x = (ctx // 2) % 4
    group = ctx // GROUP
    chip = (ctx // 2) % CHIPS
    half = z % 2
    block = half * (15 - 2 * group) + group

    def ctx_of(chip_to, core_to):
        return group * GROUP + chip_to * 2 + core_to

    def ctx_at(z_to, core_to):
        return z_to * 8 + x * 2 + core_to

    sibling = ctx_of(chip, 1 - core)
    z_right = (z + 1) % RING
    z_left = (z + RING - 1) % RING

    barrier = pltpu.get_barrier_semaphore()

    def greet(ctx_to, y_to):
        pl.semaphore_signal(barrier, inc=1, device_id=(ctx_to, y_to), device_id_type=MESH)

    def greet_chip(r, carry):
        chip_to = (chip + r) % CHIPS
        greet(ctx_of(chip_to, core), y)
        greet(ctx_of(chip_to, core), (y + 1) % 4)
        greet(ctx_of(chip_to, core), (y + 2) % 4)
        greet(ctx_of(chip_to, core), (y + 3) % 4)
        greet(ctx_of(chip_to, 1 - core), y)
        return carry

    lax.fori_loop(1, CHIPS, greet_chip, 0)
    greet(sibling, y)
    for step in range(1, 4):
        greet(ctx, (y + step) % 4)
    z_far = (z + half * 2 - 1 + RING) % RING
    greet(ctx_at(z_far, core), y)

    w_rows = w_hbm.shape[0]
    w_cols = wbuf.shape[1]
    half_rows = w_rows // 2
    own_w = pltpu.make_async_copy(
        w_hbm.at[:, pl.ds(pl.multiple_of(y * w_cols, w_cols), w_cols)],
        wbuf.at[pl.ds(pl.multiple_of(y * w_rows, w_rows), w_rows), :],
        l_w,
    )
    own_w.start()

    for hf in range(2):
        piece = ctx if hf == 0 else 255 - ctx
        row = chosen_ref[pl.ds(piece // GROUP, 1), :]
        by_rank, by_token = one_hots(row, piece * PIECE)
        picks = dot_nt(by_rank, by_token)
        pick_bf = picks.astype(BF16)
        place[hf] = dot_nt(by_token, by_rank).astype(BF16)
        rows = slice(hf * PIECE, (hf + 1) * PIECE)
        rsel[hf * MOST : (hf + 1) * MOST, :] = jnp.sum(
            picks * router_ref[:, rows].astype(F32), axis=1, keepdims=True
        )
        for kind, ref in enumerate((k_ref, v_ref, q_ref)):
            picked = jnp.dot(pick_bf, ref[rows, :], preferred_element_type=F32).astype(BF16)
            for head in range(4):
                sel[kind, hf * 4 + head] = picked[:, head * HD : (head + 1) * HD]

    pl.semaphore_wait(barrier, 40)

    my_rows = pl.ds(pl.multiple_of((chip * 2 + core) * MOST, MOST), MOST)
    my_q_rows = pl.ds(pl.multiple_of(chip * MOST, MOST), MOST)

    def first_kv(chip_to, core_to):
        return pltpu.make_async_remote_copy(
            src_ref=sel.at[core_to, chip_to],
            dst_ref=kvpad.at[my_rows, :],
            send_sem=s1, recv_sem=r1_kv,
            device_id=(ctx_of(chip_to, core_to), y), device_id_type=MESH,
        )

    def first_q(chip_to):
        return pltpu.make_async_remote_copy(
            src_ref=sel.at[2, chip_to],
            dst_ref=qpad.at[my_q_rows, :],
            send_sem=s1, recv_sem=r1_q,
            device_id=(ctx_of(chip_to, core), y), device_id_type=MESH,
        )

    first_kv(chip, 1 - core).start()

    def first_sends(r, carry):
        chip_to = (chip + r) % CHIPS
        first_kv(chip_to, core).start()
        first_kv(chip_to, 1 - core).start()
        first_q(chip_to).start()
        return carry

    lax.fori_loop(1, CHIPS, first_sends, 0)
    kvpad[my_rows, :] = sel[core, chip]
    qpad[my_q_rows, :] = sel[2, chip]

    def weights(step):
        y_to = (y + step) % 4
        return pltpu.make_async_remote_copy(
            src_ref=w_hbm.at[
                pl.ds(pl.multiple_of(core * half_rows, half_rows), half_rows),
                pl.ds(pl.multiple_of(y_to * w_cols, w_cols), w_cols),
            ],
            dst_ref=wbuf.at[
                pl.ds(pl.multiple_of(y * w_rows + core * half_rows, half_rows), half_rows), :
            ],
            send_sem=s_w, recv_sem=r_w.at[step - 1],
            device_id=(ctx, y_to), device_id_type=MESH,
        )

    for step in (1, 3, 2):
        weights(step).start()

    row = chosen_ref[pl.ds(block, 1), :]
    diagonal = lax.broadcasted_iota(jnp.int32, (PICK, PICK), 0) == lax.broadcasted_iota(
        jnp.int32, (PICK, PICK), 1
    )
    column = jnp.sum(jnp.where(diagonal, row, 0), axis=1, keepdims=True)

    def base_of(device):
        return block * 2048 + (half * 15 + (1 - 2 * half) * device) * PIECE

    slot = lax.broadcasted_iota(jnp.int32, (1, GROUP * MOST), 1)
    base = base_of(slot // MOST)
    first = jnp.sum((column < base).astype(jnp.int32), axis=0, keepdims=True)
    inside = (column >= base) & (column < base + PIECE)
    entry = lax.broadcasted_iota(jnp.int32, (PICK, GROUP * MOST), 0)
    pick[...] = ((entry - first == slot % MOST) & inside).astype(F32).astype(BF16)
    q_slot = lax.broadcasted_iota(jnp.int32, (CHIPS * MOST, 1), 0)
    q_base = base_of(q_slot // MOST * 2 + core)
    q_place = jnp.sum((row < q_base).astype(jnp.int32), axis=1, keepdims=True) + q_slot % MOST

    pltpu.make_async_copy(kv.at[pl.ds(0, 15 * MOST), :], kv.at[pl.ds(0, 15 * MOST), :], r1_kv).wait()

    def rows_of(kind, z_from, sub=None):
        if sub is None:
            return pl.ds(pl.multiple_of((kind * RING + z_from) * PICK, PICK), PICK)
        return pl.ds(pl.multiple_of((kind * RING + z_from) * PICK + sub * SUB, SUB), SUB)

    kv[rows_of(core, z), :] = jnp.dot(
        pick[...], kvpad[...], preferred_element_type=F32
    ).astype(BF16)

    def to_right(z_from, sub, step):
        rows = rows_of(core, z_from, sub)
        return pltpu.make_async_remote_copy(
            src_ref=kv.at[rows, :], dst_ref=kv.at[rows, :],
            send_sem=s2, recv_sem=r2_right.at[step * SUBS + sub],
            device_id=(ctx_at(z_right, core), y), device_id_type=MESH,
        )

    def to_left(z_from, sub, step):
        rows = rows_of(core, z_from, sub)
        return pltpu.make_async_remote_copy(
            src_ref=kv.at[rows, :], dst_ref=kv.at[rows, :],
            send_sem=s2, recv_sem=r2_left.at[step * SUBS + sub],
            device_id=(ctx_at(z_left, core), y), device_id_type=MESH,
        )

    def to_sibling(z_from):
        rows = rows_of(core, z_from)
        return pltpu.make_async_remote_copy(
            src_ref=kv.at[rows, :], dst_ref=kv.at[rows, :],
            send_sem=s_sib, recv_sem=r_sib.at[z_from],
            device_id=(sibling, y), device_id_type=MESH,
        )

    for sub in range(SUBS):
        to_right(z, sub, 0).start()
        to_left(z, sub, 0).start()
    to_sibling(z).start()

    pltpu.make_async_copy(kv.at[pl.ds(0, 7 * MOST), :], kv.at[pl.ds(0, 7 * MOST), :], r1_q).wait()

    scale = HD**-0.5 * 1.4426950408889634

    def from_sibling(z_from):
        rows = rows_of(1 - core, z_from)
        pltpu.make_async_copy(kv.at[rows, :], kv.at[rows, :], r_sib.at[z_from]).wait()

    def attend_own():
        from_sibling(z)
        scores = dot_nt(qpad[...], kv[rows_of(0, z), :]) * scale
        seen = lax.broadcasted_iota(jnp.int32, (PICK, PICK), 1) <= q_place
        scores = jnp.where(seen, scores, -1e30)
        top_now = jnp.max(scores, axis=1, keepdims=True)
        weight = jnp.exp2(scores - top_now)
        top[...] = top_now
        total[...] = jnp.sum(weight, axis=1, keepdims=True)
        acc[...] = jnp.dot(weight.astype(BF16), kv[rows_of(1, z), :], preferred_element_type=F32)

    def attend(z_from):
        from_sibling(z_from)
        half_from = z_from % 2
        block_from = half_from * 15 + (1 - 2 * half_from) * (z_from // 2)

        @pl.when(block_from < block)
        def _():
            scores = dot_nt(qpad[...], kv[rows_of(0, z_from), :]) * scale
            top_was = top[...]
            top_now = jnp.maximum(top_was, jnp.max(scores, axis=1, keepdims=True))
            weight = jnp.exp2(scores - top_now)
            fade = jnp.exp2(top_was - top_now)
            top[...] = top_now
            total[...] = total[...] * fade + jnp.sum(weight, axis=1, keepdims=True)
            acc[...] = acc[...] * fade + jnp.dot(
                weight.astype(BF16), kv[rows_of(1, z_from), :], preferred_element_type=F32
            )

    def ring_step(step, carry):
        from_left = (z + RING - step) % RING
        from_right = (z + step) % RING
        for sub in range(SUBS):
            rows = rows_of(core, from_left, sub)
            pltpu.make_async_copy(
                kv.at[rows, :], kv.at[rows, :], r2_right.at[(step - 1) * SUBS + sub]
            ).wait()
            if sub < SUBS // 2:
                to_right(from_left, sub, step).start()
            else:

                @pl.when(step < 7)
                def _():
                    to_right(from_left, sub, step).start()

            rows = rows_of(core, from_right, sub)
            pltpu.make_async_copy(
                kv.at[rows, :], kv.at[rows, :], r2_left.at[(step - 1) * SUBS + sub]
            ).wait()
            if sub >= SUBS // 2:
                to_left(from_right, sub, step).start()
            else:

                @pl.when(step < 7)
                def _():
                    to_left(from_right, sub, step).start()

        to_sibling(from_left).start()
        to_sibling(from_right).start()

        @pl.when(step == 1)
        def _():
            attend_own()

        @pl.when(step > 1)
        def _():
            attend((z + RING - step + 1) % RING)
            attend((z + step - 1) % RING)

        return carry

    lax.fori_loop(1, 8, ring_step, 0)
    z_last = (z + 8) % RING
    for sub in range(SUBS):
        rows = rows_of(core, z_last, sub)
        sem = r2_right if sub < SUBS // 2 else r2_left
        pltpu.make_async_copy(kv.at[rows, :], kv.at[rows, :], sem.at[7 * SUBS + sub]).wait()
    to_sibling(z_last).start()
    attend((z + RING - 7) % RING)
    attend((z + 7) % RING)
    attend(z_last)

    osend[...] = (acc[...] / total[...]).astype(BF16)

    att_rows = pl.ds(pl.multiple_of(half * MOST, MOST), MOST)
    att_cols = pl.ds(pl.multiple_of((y * 4 + x) * HD, HD), HD)

    def back(chip_to, y_to):
        return pltpu.make_async_remote_copy(
            src_ref=osend.at[pl.ds(pl.multiple_of(chip_to * MOST, MOST), MOST), :],
            dst_ref=att.at[att_rows, att_cols],
            send_sem=s3, recv_sem=r3,
            device_id=(ctx_of(chip_to, core), y_to), device_id_type=MESH,
        )

    for step in range(1, 4):
        back(chip, (y + step) % 4).start()

    def backs(r, carry):
        chip_to = (chip + r) % CHIPS
        for step in range(4):
            back(chip_to, (y + step) % 4).start()
        return carry

    lax.fori_loop(1, CHIPS, backs, 0)
    att[att_rows, att_cols] = osend[my_q_rows, :]

    def pass_on(step):
        y_from = (y + 4 - step) % 4
        rows = pl.ds(pl.multiple_of(y_from * w_rows + core * half_rows, half_rows), half_rows)
        pltpu.make_async_copy(wbuf.at[rows, :], wbuf.at[rows, :], r_w.at[step - 1]).wait()
        pltpu.make_async_remote_copy(
            src_ref=wbuf.at[rows, :], dst_ref=wbuf.at[rows, :],
            send_sem=s_wf, recv_sem=r_wf,
            device_id=(sibling, y), device_id_type=MESH,
        ).start()

    for step in (1, 3, 2):
        pass_on(step)
    own_w.wait()
    three = wbuf.at[pl.ds(0, 3 * half_rows), :]
    pltpu.make_async_copy(three, three, r_wf).wait()
    pltpu.make_async_copy(kv.at[pl.ds(0, 31 * MOST), :], kv.at[pl.ds(0, 31 * MOST), :], r3).wait()

    updates = jnp.dot(att[...], wbuf[...], preferred_element_type=F32) * rsel[...]
    updates = updates.astype(BF16)
    for hf in range(2):
        out_ref[hf * PIECE : (hf + 1) * PIECE, :] = jnp.dot(
            place[hf], updates[hf * MOST : (hf + 1) * MOST, :], preferred_element_type=F32
        ).astype(BF16)

    sent = kv.at[pl.ds(0, 22 * MOST), :]
    pltpu.make_async_copy(sent, sent, s1).wait()
    sent = kv.at[pl.ds(0, 15 * PICK), :]
    pltpu.make_async_copy(sent, sent, s2).wait()
    sent = kv.at[pl.ds(0, 16 * PICK), :]
    pltpu.make_async_copy(sent, sent, s_sib).wait()
    sent = kv.at[pl.ds(0, 31 * MOST), :]
    pltpu.make_async_copy(sent, sent, s3).wait()
    pltpu.make_async_copy(three, three, s_w).wait()
    pltpu.make_async_copy(three, three, s_wf).wait()


def shards(queries, key_proj, value_proj, router, chosen, out_weight):
    tok_rows = queries.shape[0]
    w_cols = out_weight.shape[1] // 4
    dma = pltpu.SemaphoreType.DMA
    vmem = pl.BlockSpec(memory_space=pltpu.VMEM)
    return pl.pallas_call(
        body,
        out_shape=jax.ShapeDtypeStruct((tok_rows, w_cols), BF16),
        in_specs=[vmem] * 5 + [pl.BlockSpec(memory_space=pl.ANY)],
        out_specs=vmem,
        scratch_shapes=[
            pltpu.VMEM((3, CHIPS, MOST, HD), BF16),
            pltpu.VMEM((GROUP * MOST, HD), BF16),
            pltpu.VMEM((CHIPS * MOST, HD), BF16),
            pltpu.VMEM((2 * RING * PICK, HD), BF16),
            pltpu.VMEM((2 * MOST, 16 * HD), BF16),
            pltpu.VMEM((CHIPS * MOST, HD), BF16),
            pltpu.VMEM((4 * out_weight.shape[0], w_cols), BF16),
            pltpu.VMEM((2, PIECE, MOST), BF16),
            pltpu.VMEM((2 * MOST, 1), F32),
            pltpu.VMEM((CHIPS * MOST, 1), F32),
            pltpu.VMEM((CHIPS * MOST, 1), F32),
            pltpu.VMEM((CHIPS * MOST, HD), F32),
            pltpu.VMEM((PICK, GROUP * MOST), BF16),
            dma, dma, dma,
            dma, dma((8 * SUBS,)), dma((8 * SUBS,)),
            dma, dma((RING,)),
            dma, dma,
            dma, dma((3,)), dma, dma, dma,
        ],
        compiler_params=pltpu.CompilerParams(
            collective_id=0, has_side_effects=True, vmem_limit_bytes=40 * 1024 * 1024
        ),
        name="routed_attention",
    )(queries, key_proj, value_proj, router.reshape(1, tok_rows), chosen, out_weight)


def solution(mesh):
    placed = (P("ctx", "tp"), P("ctx", "tp"), P("ctx", "tp"), P("ctx"), P(), P("tp", None))
    return jax.shard_map(
        shards, mesh=mesh, in_specs=placed, out_specs=P("ctx", "tp"), check_vma=False
    )
```

time: 621 us -> 62.2 us (0.10)
  blocking collectives: 499 us -> 0 us
  Pallas kernels: 0 us -> 54.7 us
  local copies, waits for them, and re-layouts: 41.6 us -> 7.21 us
  matrix products: 24.1 us -> 0 us
  waiting for transfers between devices: 24 us -> 0 us
  between operations: 18.1 us -> 0.01 us
  other arithmetic: 13 us -> 0 us
    unnamed x1 -> x0, blocking collectives: 499 us -> none
    pallas_call x0 -> x1, Pallas kernels: none -> 54.7 us  [shards(): pl.pallas_call(body, out_shape=jax.ShapeDtypeStruct((tok_rows, w_cols), B...]
    slice x3 -> x0, local copies, waits for them, and re-layouts: 34 us -> none  [the longest x2 22.7 us: attend(): key_part = pair_part[:, 0].reshape(part_rows, head_count, HD)]
    dot_general x4 -> x0, matrix products: 24.1 us -> none  [the longest x1 9.29 us: attend(): jnp.einsum('qhd,khd->hqk', shaped, key_part, preferred_element_type=jnp.f...]
    reduce_scatter x1 -> x0, waiting for transfers between devices: 23.9 us -> none  [project(): lax.psum_scatter(lax.dot_general(out_weight, attended, (((0,), (1,)), (()...]
    reduce_sum x3 -> x0, other arithmetic: 6.77 us -> none  [the longest x1 5.34 us: attend(): total_new = jnp.sum(weights, axis=2)]
  transfers between devices with their start and end apart: 2 -> 0, of which waited for: 1 -> 0; matrix products, arithmetic and copies ran while one was open for 1% -> 0% of each run, Pallas kernels for 0% -> 0%
where the time goes in v1:
time: 62.2 us; the launch traced here: 61.9 us
  Pallas kernels  54.7 us (88%)
  local copies, waits for them, and re-layouts  7.21 us (12%)
    pallas_call x1, Pallas kernels, shards(): pl.pallas_call(body, out_shape=jax.ShapeDtypeStruct((tok_rows, w_cols), B...  54.7 us
    unnamed x11, local copies, waits for them, and re-layouts  6.55 us

profile of v1, /device:TPU:1, one launch (start us, length us, event | category | flops | bytes accessed | tf_op | source)
XLA Modules:
  0.0 61.9 jit_solution(7119130875323112619)
XLA Ops:
  0.0 0.7 %reshape.3.router_ref = bf16[1,256]{1,0:T(2,128)(2,1)S(1)} reshape(bf16[256]{0:T(256)(128)(2,1)} %param.9) | data formatting | bytes 1024 | tf_op jit(solution)/shard_map/reshape | solution.py:405
  0.7 0.0 copy-start
  0.7 2.2 %copy-done = bf16[512,4096]{1,0:T(8,128)(2,1)S(1)} copy-done((bf16[512,4096]{1,0:T(8,128)(2,1)S(1)}, bf16[512,4096]{1,0:T(8,128)(2,1)}, u32[]{:S(2)}) %copy-start) | copy-done | bytes 4194328
  2.8 0.0 copy-start.1
  2.8 0.9 %copy-done.1 = bf16[256,512]{1,0:T(8,128)(2,1)S(1)} copy-done((bf16[256,512]{1,0:T(8,128)(2,1)S(1)}, bf16[256,512]{1,0:T(8,128)(2,1)}, u32[]{:S(2)}) %copy-start.1) | copy-done | bytes 262168
  3.8 0.0 copy-start.2
  3.8 0.9 %copy-done.2 = bf16[256,512]{1,0:T(8,128)(2,1)S(1)} copy-done((bf16[256,512]{1,0:T(8,128)(2,1)S(1)}, bf16[256,512]{1,0:T(8,128)(2,1)}, u32[]{:S(2)}) %copy-start.2) | copy-done | bytes 262168
  4.7 0.0 copy-start.3
  4.8 0.9 %copy-done.3 = bf16[256,512]{1,0:T(8,128)(2,1)S(1)} copy-done((bf16[256,512]{1,0:T(8,128)(2,1)S(1)}, bf16[256,512]{1,0:T(8,128)(2,1)}, u32[]{:S(2)}) %copy-start.3) | copy-done | bytes 262168
  5.7 0.0 copy-start.4
  5.7 0.7 %copy-done.4 = s32[16,256]{1,0:T(8,128)S(1)} copy-done((s32[16,256]{1,0:T(8,128)S(1)}, s32[16,256]{1,0:T(8,128)}, u32[]{:S(2)}) %copy-start.4) | copy-done | bytes 16408
  6.4 54.7 %routed_attention.1 = bf16[256,1024]{1,0:T(8,128)(2,1)S(1)} custom-call(bf16[256,512]{1,0:T(8,128)(2,1)S(1)} %copy-done.1, bf16[256,512]{1,0:T(8,128)(2,1)S(1)} %copy-done.2, bf16[256,512]{1,0:T(8,128)(2,1)S(1)} %copy-done.3, bf16[1,256]{1,0:T(2,128)(2,1)S(1)} %reshape.3.router_ref, s32[16,256]{1,0:T(8,128)S(1)} %copy-done.4, bf16[512,4096]{1,0:T(8,128)(2,1)S(1)} %copy-done), custom_call_target="tpu_custom_call" | custom-call | tf_op jit(solution)/shard_map/routed_attention/pallas_call | solution.py:376
  61.1 0.8 %copy.8 = bf16[256,1024]{1,0:T(8,128)(2,1)} copy(bf16[256,1024]{1,0:T(8,128)(2,1)S(1)} %routed_attention.1) | data formatting | bytes 1048576
Async XLA Ops:
  0.7 2.2 %copy-start = (bf16[512,4096]{1,0:T(8,128)(2,1)S(1)}, bf16[512,4096]{1,0:T(8,128)(2,1)}, u32[]{:S(2)}) copy-start(bf16[512,4096]{1,0:T(8,128)(2,1)} %w_hbm.1) | copy-start | bytes 12582916
  2.8 0.9 %copy-start.1 = (bf16[256,512]{1,0:T(8,128)(2,1)S(1)}, bf16[256,512]{1,0:T(8,128)(2,1)}, u32[]{:S(2)}) copy-start(bf16[256,512]{1,0:T(8,128)(2,1)} %q_ref.1) | copy-start | bytes 786436
  3.8 0.9 %copy-start.2 = (bf16[256,512]{1,0:T(8,128)(2,1)S(1)}, bf16[256,512]{1,0:T(8,128)(2,1)}, u32[]{:S(2)}) copy-start(bf16[256,512]{1,0:T(8,128)(2,1)} %k_ref.1) | copy-start | bytes 786436
  4.7 0.9 %copy-start.3 = (bf16[256,512]{1,0:T(8,128)(2,1)S(1)}, bf16[256,512]{1,0:T(8,128)(2,1)}, u32[]{:S(2)}) copy-start(bf16[256,512]{1,0:T(8,128)(2,1)} %v_ref.1) | copy-start | bytes 786436
  5.7 0.7 %copy-start.4 = (s32[16,256]{1,0:T(8,128)S(1)}, s32[16,256]{1,0:T(8,128)}, u32[]{:S(2)}) copy-start(s32[16,256]{1,0:T(8,128)} %chosen_ref.1) | copy-start | bytes 49156

commit v2 on v1

--- a/solution.py
+++ b/solution.py
@@ -13,7 +13,7 @@
 GROUP = 16
 CHIPS = 8
 RING = 16
-SUBS = 4
+SUBS = 2
 SUB = PICK // SUBS
 MESH = pl.DeviceIdType.MESH
 F32 = jnp.float32
@@ -36,9 +36,9 @@
 
 
 def body(
-    q_ref, k_ref, v_ref, router_ref, chosen_ref, w_hbm, out_ref,
-    sel, kvpad, qpad, kv, att, osend, wbuf, place, rsel, top, total, acc, pick,
-    s1, r1_kv, r1_q, s2, r2_right, r2_left, s_sib, r_sib, s3, r3, s_w, r_w, s_wf, r_wf, l_w,
+    q_hbm, k_hbm, v_hbm, router_ref, chosen_hbm, w_hbm, out_ref,
+    q_ref, k_ref, v_ref, chosen_ref, l_in, sel, pad_own, pad_other, kv, att, osend, wbuf, place, rsel, top, total, acc, pick,
+    s1, r1_own, r1_other, s2, r2_far_right, r2_far_left, r2_near_right, r2_near_left, s_sib, r_sib, s3, r3, s_w, r_w, s_wf, r_wf, l_w,
 ):
     ctx = lax.axis_index("ctx")
     y = lax.axis_index("tp")
@@ -60,6 +60,15 @@
     z_right = (z + 1) % RING
     z_left = (z + RING - 1) % RING
 
+    loads = [
+        pltpu.make_async_copy(src, dst, l_in.at[n])
+        for n, (src, dst) in enumerate(
+            ((chosen_hbm, chosen_ref), (k_hbm, k_ref), (v_hbm, v_ref), (q_hbm, q_ref))
+        )
+    ]
+    for load in loads:
+        load.start()
+
     barrier = pltpu.get_barrier_semaphore()
 
     def greet(ctx_to, y_to):
@@ -68,9 +77,6 @@
     def greet_chip(r, carry):
         chip_to = (chip + r) % CHIPS
         greet(ctx_of(chip_to, core), y)
-        greet(ctx_of(chip_to, core), (y + 1) % 4)
-        greet(ctx_of(chip_to, core), (y + 2) % 4)
-        greet(ctx_of(chip_to, core), (y + 3) % 4)
         greet(ctx_of(chip_to, 1 - core), y)
         return carry
 
@@ -78,8 +84,9 @@
     greet(sibling, y)
     for step in range(1, 4):
         greet(ctx, (y + step) % 4)
-    z_far = (z + half * 2 - 1 + RING) % RING
-    greet(ctx_at(z_far, core), y)
+    greet(ctx_at((z + half * 2 - 1 + RING) % RING, core), y)
+    greet(ctx_at((z + 2) % RING, core), y)
+    greet(ctx_at((z + RING - 2) % RING, core), y)
 
     w_rows = w_hbm.shape[0]
     w_cols = wbuf.shape[1]
@@ -90,6 +97,9 @@
         l_w,
     )
     own_w.start()
+
+    for load in loads:
+        load.wait()
 
     for hf in range(2):
         piece = ctx if hf == 0 else 255 - ctx
@@ -102,44 +112,40 @@
         rsel[hf * MOST : (hf + 1) * MOST, :] = jnp.sum(
             picks * router_ref[:, rows].astype(F32), axis=1, keepdims=True
         )
-        for kind, ref in enumerate((k_ref, v_ref, q_ref)):
+        for kind, ref in ((1 - core, k_ref), (core, v_ref), (2, q_ref)):
             picked = jnp.dot(pick_bf, ref[rows, :], preferred_element_type=F32).astype(BF16)
             for head in range(4):
-                sel[kind, hf * 4 + head] = picked[:, head * HD : (head + 1) * HD]
-
-    pl.semaphore_wait(barrier, 40)
-
-    my_rows = pl.ds(pl.multiple_of((chip * 2 + core) * MOST, MOST), MOST)
+                sel[hf * 4 + head, kind] = picked[:, head * HD : (head + 1) * HD]
+
+    pl.semaphore_wait(barrier, 21)
+
     my_q_rows = pl.ds(pl.multiple_of(chip * MOST, MOST), MOST)
 
-    def first_kv(chip_to, core_to):
-        return pltpu.make_async_remote_copy(
-            src_ref=sel.at[core_to, chip_to],
-            dst_ref=kvpad.at[my_rows, :],
-            send_sem=s1, recv_sem=r1_kv,
-            device_id=(ctx_of(chip_to, core_to), y), device_id_type=MESH,
-        )
-
-    def first_q(chip_to):
-        return pltpu.make_async_remote_copy(
-            src_ref=sel.at[2, chip_to],
-            dst_ref=qpad.at[my_q_rows, :],
-            send_sem=s1, recv_sem=r1_q,
+    def first_own(chip_to):
+        return pltpu.make_async_remote_copy(
+            src_ref=sel.at[chip_to, pl.ds(1, 2)],
+            dst_ref=pad_own.at[chip],
+            send_sem=s1, recv_sem=r1_own,
             device_id=(ctx_of(chip_to, core), y), device_id_type=MESH,
         )
 
-    first_kv(chip, 1 - core).start()
+    def first_other(chip_to):
+        return pltpu.make_async_remote_copy(
+            src_ref=sel.at[chip_to, 0],
+            dst_ref=pad_other.at[chip],
+            send_sem=s1, recv_sem=r1_other,
+            device_id=(ctx_of(chip_to, 1 - core), y), device_id_type=MESH,
+        )
 
     def first_sends(r, carry):
         chip_to = (chip + r) % CHIPS
-        first_kv(chip_to, core).start()
-        first_kv(chip_to, 1 - core).start()
-        first_q(chip_to).start()
+        first_own(chip_to).start()
+        first_other(chip_to).start()
         return carry
 
     lax.fori_loop(1, CHIPS, first_sends, 0)
-    kvpad[my_rows, :] = sel[core, chip]
-    qpad[my_q_rows, :] = sel[2, chip]
+    first_other(chip).start()
+    pad_own[chip] = sel[chip, 1:3]
 
     def weights(step):
         y_to = (y + step) % 4
@@ -168,7 +174,8 @@
         return block * 2048 + (half * 15 + (1 - 2 * half) * device) * PIECE
 
     slot = lax.broadcasted_iota(jnp.int32, (1, GROUP * MOST), 1)
-    base = base_of(slot // MOST)
+    slot_core = (core + slot // (CHIPS * MOST)) % 2
+    base = base_of(slot // MOST % CHIPS * 2 + slot_core)
     first = jnp.sum((column < base).astype(jnp.int32), axis=0, keepdims=True)
     inside = (column >= base) & (column < base + PIECE)
     entry = lax.broadcasted_iota(jnp.int32, (PICK, GROUP * MOST), 0)
@@ -177,32 +184,44 @@
     q_base = base_of(q_slot // MOST * 2 + core)
     q_place = jnp.sum((row < q_base).astype(jnp.int32), axis=1, keepdims=True) + q_slot % MOST
 
-    pltpu.make_async_copy(kv.at[pl.ds(0, 15 * MOST), :], kv.at[pl.ds(0, 15 * MOST), :], r1_kv).wait()
+    arrived = pad_own.at[pl.ds(0, CHIPS - 1)]
+    pltpu.make_async_copy(arrived, arrived, r1_own).wait()
+    pltpu.make_async_copy(pad_other, pad_other, r1_other).wait()
 
     def rows_of(kind, z_from, sub=None):
         if sub is None:
             return pl.ds(pl.multiple_of((kind * RING + z_from) * PICK, PICK), PICK)
         return pl.ds(pl.multiple_of((kind * RING + z_from) * PICK + sub * SUB, SUB), SUB)
 
-    kv[rows_of(core, z), :] = jnp.dot(
-        pick[...], kvpad[...], preferred_element_type=F32
-    ).astype(BF16)
-
-    def to_right(z_from, sub, step):
+    own_side = jnp.dot(
+        pick[:, : CHIPS * MOST],
+        pad_own[:, 0].reshape(CHIPS * MOST, HD),
+        preferred_element_type=F32,
+    )
+    other_side = jnp.dot(
+        pick[:, CHIPS * MOST :],
+        pad_other[...].reshape(CHIPS * MOST, HD),
+        preferred_element_type=F32,
+    )
+    kv[rows_of(core, z), :] = (own_side + other_side).astype(BF16)
+
+    def carry_on(z_from, sub, level, way, reach, sems):
         rows = rows_of(core, z_from, sub)
         return pltpu.make_async_remote_copy(
             src_ref=kv.at[rows, :], dst_ref=kv.at[rows, :],
-            send_sem=s2, recv_sem=r2_right.at[step * SUBS + sub],
-            device_id=(ctx_at(z_right, core), y), device_id_type=MESH,
-        )
-
-    def to_left(z_from, sub, step):
+            send_sem=s2, recv_sem=sems.at[level * SUBS + sub],
+            device_id=(ctx_at((z + RING + way * reach) % RING, core), y), device_id_type=MESH,
+        )
+
+    def far(z_from, sub, level, way):
+        return carry_on(z_from, sub, level, way, 2, r2_far_right if way > 0 else r2_far_left)
+
+    def near(z_from, sub, level, way):
+        return carry_on(z_from, sub, level, way, 1, r2_near_right if way > 0 else r2_near_left)
+
+    def arrive(z_from, sub, level, sems):
         rows = rows_of(core, z_from, sub)
-        return pltpu.make_async_remote_copy(
-            src_ref=kv.at[rows, :], dst_ref=kv.at[rows, :],
-            send_sem=s2, recv_sem=r2_left.at[step * SUBS + sub],
-            device_id=(ctx_at(z_left, core), y), device_id_type=MESH,
-        )
+        pltpu.make_async_copy(kv.at[rows, :], kv.at[rows, :], sems.at[level * SUBS + sub]).wait()
 
     def to_sibling(z_from):
         rows = rows_of(core, z_from)
@@ -212,12 +231,11 @@
             device_id=(sibling, y), device_id_type=MESH,
         )
 
-    for sub in range(SUBS):
-        to_right(z, sub, 0).start()
-        to_left(z, sub, 0).start()
+    for send in (far, near):
+        for sub in range(SUBS):
+            send(z, sub, 0, 1).start()
+            send(z, sub, 0, -1).start()
     to_sibling(z).start()
-
-    pltpu.make_async_copy(kv.at[pl.ds(0, 7 * MOST), :], kv.at[pl.ds(0, 7 * MOST), :], r1_q).wait()
 
     scale = HD**-0.5 * 1.4426950408889634
 
@@ -227,7 +245,7 @@
 
     def attend_own():
         from_sibling(z)
-        scores = dot_nt(qpad[...], kv[rows_of(0, z), :]) * scale
+        scores = dot_nt(pad_own[:, 1].reshape(CHIPS * MOST, HD), kv[rows_of(0, z), :]) * scale
         seen = lax.broadcasted_iota(jnp.int32, (PICK, PICK), 1) <= q_place
         scores = jnp.where(seen, scores, -1e30)
         top_now = jnp.max(scores, axis=1, keepdims=True)
@@ -243,7 +261,7 @@
 
         @pl.when(block_from < block)
         def _():
-            scores = dot_nt(qpad[...], kv[rows_of(0, z_from), :]) * scale
+            scores = dot_nt(pad_own[:, 1].reshape(CHIPS * MOST, HD), kv[rows_of(0, z_from), :]) * scale
             top_was = top[...]
             top_now = jnp.maximum(top_was, jnp.max(scores, axis=1, keepdims=True))
             weight = jnp.exp2(scores - top_now)
@@ -254,57 +272,72 @@
                 weight.astype(BF16), kv[rows_of(1, z_from), :], preferred_element_type=F32
             )
 
-    def ring_step(step, carry):
-        from_left = (z + RING - step) % RING
-        from_right = (z + step) % RING
+    def level_step(level, carry):
+        from_left = (z + RING - 2 * level) % RING
+        from_right = (z + 2 * level) % RING
         for sub in range(SUBS):
-            rows = rows_of(core, from_left, sub)
-            pltpu.make_async_copy(
-                kv.at[rows, :], kv.at[rows, :], r2_right.at[(step - 1) * SUBS + sub]
-            ).wait()
+            arrive(from_left, sub, level - 1, r2_far_right)
             if sub < SUBS // 2:
-                to_right(from_left, sub, step).start()
+                far(from_left, sub, level, 1).start()
             else:
 
-                @pl.when(step < 7)
+                @pl.when(level < 3)
                 def _():
-                    to_right(from_left, sub, step).start()
-
-            rows = rows_of(core, from_right, sub)
-            pltpu.make_async_copy(
-                kv.at[rows, :], kv.at[rows, :], r2_left.at[(step - 1) * SUBS + sub]
-            ).wait()
+                    far(from_left, sub, level, 1).start()
+
+            arrive(from_right, sub, level - 1, r2_far_left)
             if sub >= SUBS // 2:
-                to_left(from_right, sub, step).start()
+                far(from_right, sub, level, -1).start()
             else:
 
-                @pl.when(step < 7)
+                @pl.when(level < 3)
                 def _():
-                    to_left(from_right, sub, step).start()
-
+                    far(from_right, sub, level, -1).start()
+
+        for sub in range(SUBS):
+            near(from_left, sub, level, 1).start()
+            near(from_right, sub, level, -1).start()
         to_sibling(from_left).start()
         to_sibling(from_right).start()
-
-        @pl.when(step == 1)
+        next_left = (z + RING - 2 * level + 1) % RING
+        next_right = (z + 2 * level - 1) % RING
+        for sub in range(SUBS):
+            arrive(next_left, sub, level - 1, r2_near_right)
+            arrive(next_right, sub, level - 1, r2_near_left)
+        to_sibling(next_left).start()
+        to_sibling(next_right).start()
+
+        @pl.when(level == 1)
         def _():
             attend_own()
 
-        @pl.when(step > 1)
+        @pl.when(level > 1)
         def _():
-            attend((z + RING - step + 1) % RING)
-            attend((z + step - 1) % RING)
+            attend_level(level - 1)
 
         return carry
 
-    lax.fori_loop(1, 8, ring_step, 0)
+    def attend_level(level):
+        attend((z + RING - 2 * level + 1) % RING)
+        attend((z + 2 * level - 1) % RING)
+        attend((z + RING - 2 * level) % RING)
+        attend((z + 2 * level) % RING)
+
+    lax.fori_loop(1, 4, level_step, 0)
     z_last = (z + 8) % RING
+    last_left = (z + RING - 7) % RING
+    last_right = (z + 7) % RING
     for sub in range(SUBS):
-        rows = rows_of(core, z_last, sub)
-        sem = r2_right if sub < SUBS // 2 else r2_left
-        pltpu.make_async_copy(kv.at[rows, :], kv.at[rows, :], sem.at[7 * SUBS + sub]).wait()
+        arrive(last_left, sub, 3, r2_near_right)
+        arrive(last_right, sub, 3, r2_near_left)
+    to_sibling(last_left).start()
+    to_sibling(last_right).start()
+    for sub in range(SUBS):
+        arrive(z_last, sub, 3, r2_far_right if sub < SUBS // 2 else r2_far_left)
     to_sibling(z_last).start()
-    attend((z + RING - 7) % RING)
-    attend((z + 7) % RING)
+    attend_level(3)
+    attend(last_left)
+    attend(last_right)
     attend(z_last)
 
     osend[...] = (acc[...] / total[...]).astype(BF16)
@@ -356,8 +389,8 @@
             place[hf], updates[hf * MOST : (hf + 1) * MOST, :], preferred_element_type=F32
         ).astype(BF16)
 
-    sent = kv.at[pl.ds(0, 22 * MOST), :]
-    pltpu.make_async_copy(sent, sent, s1).wait()
+    pltpu.make_async_copy(arrived, arrived, s1).wait()
+    pltpu.make_async_copy(pad_other, pad_other, s1).wait()
     sent = kv.at[pl.ds(0, 15 * PICK), :]
     pltpu.make_async_copy(sent, sent, s2).wait()
     sent = kv.at[pl.ds(0, 16 * PICK), :]
@@ -373,15 +406,21 @@
     w_cols = out_weight.shape[1] // 4
     dma = pltpu.SemaphoreType.DMA
     vmem = pl.BlockSpec(memory_space=pltpu.VMEM)
+    hbm = pl.BlockSpec(memory_space=pltpu.HBM)
     return pl.pallas_call(
         body,
         out_shape=jax.ShapeDtypeStruct((tok_rows, w_cols), BF16),
-        in_specs=[vmem] * 5 + [pl.BlockSpec(memory_space=pl.ANY)],
+        in_specs=[hbm] * 3 + [vmem] + [hbm] * 2,
         out_specs=vmem,
         scratch_shapes=[
-            pltpu.VMEM((3, CHIPS, MOST, HD), BF16),
-            pltpu.VMEM((GROUP * MOST, HD), BF16),
-            pltpu.VMEM((CHIPS * MOST, HD), BF16),
+            pltpu.VMEM(queries.shape, BF16),
+            pltpu.VMEM(key_proj.shape, BF16),
+            pltpu.VMEM(value_proj.shape, BF16),
+            pltpu.VMEM(chosen.shape, jnp.int32),
+            dma((4,)),
+            pltpu.VMEM((CHIPS, 3, MOST, HD), BF16),
+            pltpu.VMEM((CHIPS, 2, MOST, HD), BF16),
+            pltpu.VMEM((CHIPS, MOST, HD), BF16),
             pltpu.VMEM((2 * RING * PICK, HD), BF16),
             pltpu.VMEM((2 * MOST, 16 * HD), BF16),
             pltpu.VMEM((CHIPS * MOST, HD), BF16),
@@ -393,13 +432,13 @@
             pltpu.VMEM((CHIPS * MOST, HD), F32),
             pltpu.VMEM((PICK, GROUP * MOST), BF16),
             dma, dma, dma,
-            dma, dma((8 * SUBS,)), dma((8 * SUBS,)),
+            dma, *[dma((4 * SUBS,))] * 4,
             dma, dma((RING,)),
             dma, dma,
             dma, dma((3,)), dma, dma, dma,
         ],
         compiler_params=pltpu.CompilerParams(
-            collective_id=0, has_side_effects=True, vmem_limit_bytes=40 * 1024 * 1024
+            collective_id=0, has_side_effects=True, vmem_limit_bytes=60 * 1024 * 1024
         ),
         name="routed_attention",
     )(queries, key_proj, value_proj, router.reshape(1, tok_rows), chosen, out_weight)

time: 62.2 us -> 52.9 us (0.85)
  Pallas kernels: 54.7 us -> 49.3 us
  local copies, waits for them, and re-layouts: 7.21 us -> 3.09 us
    pallas_call x1, Pallas kernels: 54.7 us -> 49.3 us  [shards(): pl.pallas_call(body, out_shape=jax.ShapeDtypeStruct((tok_rows, w_cols), B...]
    unnamed x11 -> x1, local copies, waits for them, and re-layouts: 6.55 us -> 1.87 us
where the time goes in v2:
time: 52.9 us; the launch traced here: 52.4 us
  Pallas kernels  49.3 us (93%)
  local copies, waits for them, and re-layouts  3.09 us (6%)
    pallas_call x1, Pallas kernels, shards(): pl.pallas_call(body, out_shape=jax.ShapeDtypeStruct((tok_rows, w_cols), B...  49.3 us
    unnamed x1, local copies, waits for them, and re-layouts  1.87 us
    reshape x1, local copies, waits for them, and re-layouts, shards(): router.reshape(1, tok_rows)  1.22 us

profile of v2, /device:TPU:1, one launch (start us, length us, event | category | flops | bytes accessed | tf_op | source)
XLA Modules:
  0.0 52.4 jit_solution(475326251461901741)
XLA Ops:
  0.0 1.2 %reshape.3.router_ref = bf16[1,256]{1,0:T(2,128)(2,1)} reshape(bf16[256]{0:T(256)(128)(2,1)} %param.9) | data formatting | bytes 1024 | tf_op jit(solution)/shard_map/reshape | solution.py:444
  1.2 49.3 %routed_attention.1 = bf16[256,1024]{1,0:T(8,128)(2,1)} custom-call(bf16[256,512]{1,0:T(8,128)(2,1)} %q_hbm.1, bf16[256,512]{1,0:T(8,128)(2,1)} %k_hbm.1, bf16[256,512]{1,0:T(8,128)(2,1)} %v_hbm.1, bf16[1,256]{1,0:T(2,128)(2,1)} %reshape.3.router_ref, s32[16,256]{1,0:T(8,128)} %chosen_hbm.1, bf16[512,4096]{1,0:T(8,128)(2,1)} %w_hbm.1), custom_call_target="tpu_custom_call" | custom-call | tf_op jit(solution)/shard_map/routed_attention/pallas_call | solution.py:410
  50.6 1.9 %copy.8 = bf16[256,1024]{1,0:T(8,128)(2,1)} copy(bf16[256,1024]{1,0:T(8,128)(2,1)} %routed_attention.1) | data formatting | bytes 1048576

commit v3 on v2

v3 whole, which is shorter than its diff:
```python
import functools
import jax
import jax.numpy as jnp
from jax import lax
from jax.experimental import pallas as pl
from jax.experimental.pallas import tpu as pltpu
from jax.sharding import PartitionSpec as P

HD = 128
PIECE = 128
MOST = 32
PICK = 256
GROUP = 16
CHIPS = 8
RING = 16
SUBS = 2
SUB = PICK // SUBS
EARLY = {1: 0, 3: 1, 2: 1, 5: 3, 4: 3, 7: 5, 6: 5, 8: 7}
LATE = {2: 0, 4: 2, 6: 4, 8: 6}
ORDER = (-1, -2, "own", -3, -4, 1, 2, -5, -6, 3, 4, -7, -8, 5, 6, 7, 8)
MESH = pl.DeviceIdType.MESH
F32 = jnp.float32
BF16 = jnp.bfloat16


def z_partners():
    found = (set(), set())
    for source, stops in ((0, EARLY), (1, LATE)):
        for stop, before in stops.items():
            for way in (1, -1):
                found[(source + before) % 2].add(way * (stop - before))
                found[(source + stop) % 2].add(way * (before - stop))
    return found


def one_hots(chosen_row, base):
    first = jnp.sum((chosen_row < base).astype(jnp.int32), axis=1, keepdims=True)
    inside = (chosen_row >= base) & (chosen_row < base + PIECE)
    entry = lax.broadcasted_iota(jnp.int32, (MOST, PICK), 1)
    rank = lax.broadcasted_iota(jnp.int32, (MOST, PICK), 0)
    by_rank = (entry - first == rank) & inside
    token = lax.broadcasted_iota(jnp.int32, (PIECE, PICK), 0)
    by_token = chosen_row - base == token
    return by_rank.astype(F32).astype(BF16), by_token.astype(F32).astype(BF16)


def dot_nt(a, b):
    return lax.dot_general(a, b, (((1,), (1,)), ((), ())), preferred_element_type=F32)


def body(
    q_hbm, k_hbm, v_hbm, router_hbm, chosen_hbm, w_hbm, out_ref,
    q_ref, k_ref, v_ref, router_ref, chosen_ref, l_in, sel, pad_own, pad_other, kv, att, osend, wbuf, place, rsel, top, total, acc, pick,
    s1, r1_own, r1_other, s2, r2, s_sib, r_sib, s3, r3, s_w, r_w, s_wf, r_wf, l_w,
):
    ctx = lax.axis_index("ctx")
    y = lax.axis_index("tp")
    z = ctx // 8
    core = ctx % 2
    x = (ctx // 2) % 4
    group = ctx // GROUP
    chip = (ctx // 2) % CHIPS
    half = z % 2

    def ctx_of(chip_to, core_to):
        return group * GROUP + chip_to * 2 + core_to

    def ctx_at(z_to, core_to):
        return z_to * 8 + x * 2 + core_to

    sibling = ctx_of(chip, 1 - core)

    def at(delta):
        return (z + RING + delta) % RING

    def block_at(z_of):
        return z_of % 2 * (15 - z_of // 2 * 2) + z_of // 2

    def needs(z_to, z_from):
        return block_at(z_from) < block_at(z_to)

    block = block_at(z)
    loads = [
        pltpu.make_async_copy(src, dst, l_in.at[n])
        for n, (src, dst) in enumerate(
            ((chosen_hbm, chosen_ref), (k_hbm, k_ref), (v_hbm, v_ref), (q_hbm, q_ref), (router_hbm, router_ref))
        )
    ]
    for load in loads:
        load.start()

    barrier = pltpu.get_barrier_semaphore()

    def greet(ctx_to, y_to):
        pl.semaphore_signal(barrier, inc=1, device_id=(ctx_to, y_to), device_id_type=MESH)

    def greet_chip(r, carry):
        chip_to = (chip + r) % CHIPS
        greet(ctx_of(chip_to, core), y)
        greet(ctx_of(chip_to, 1 - core), y)
        return carry

    lax.fori_loop(1, CHIPS, greet_chip, 0)
    greet(sibling, y)
    for step in range(1, 4):
        greet(ctx, (y + step) % 4)
    even_far, odd_far = z_partners()
    even_far -= {1}
    odd_far -= {-1}
    for delta in sorted(even_far & odd_far):
        greet(ctx_at(at(delta), core), y)

    @pl.when(half == 0)
    def _():
        for delta in sorted(even_far - odd_far):
            greet(ctx_at(at(delta), core), y)

    @pl.when(half == 1)
    def _():
        for delta in sorted(odd_far - even_far):
            greet(ctx_at(at(delta), core), y)

    w_rows = w_hbm.shape[0]
    w_cols = wbuf.shape[1]
    half_rows = w_rows // 2
    own_w = pltpu.make_async_copy(
        w_hbm.at[:, pl.ds(pl.multiple_of(y * w_cols, w_cols), w_cols)],
        wbuf.at[pl.ds(pl.multiple_of(y * w_rows, w_rows), w_rows), :],
        l_w,
    )
    own_w.start()

    for load in loads:
        load.wait()

    for hf in range(2):
        piece = ctx if hf == 0 else 255 - ctx
        row = chosen_ref[pl.ds(piece // GROUP, 1), :]
        by_rank, by_token = one_hots(row, piece * PIECE)
        picks = dot_nt(by_rank, by_token)
        pick_bf = picks.astype(BF16)
        place[hf] = dot_nt(by_token, by_rank).astype(BF16)
        rows = slice(hf * PIECE, (hf + 1) * PIECE)
        rsel[hf * MOST : (hf + 1) * MOST, :] = jnp.sum(
            picks * router_ref[rows].astype(F32).reshape(1, PIECE), axis=1, keepdims=True
        )
        for kind, ref in ((1 - core, k_ref), (core, v_ref), (2, q_ref)):
            picked = jnp.dot(pick_bf, ref[rows, :], preferred_element_type=F32).astype(BF16)
            for head in range(4):
                sel[hf * 4 + head, kind] = picked[:, head * HD : (head + 1) * HD]

    pl.semaphore_wait(barrier, 18 + len(even_far) + (len(odd_far) - len(even_far)) * half)

    my_q_rows = pl.ds(pl.multiple_of(chip * MOST, MOST), MOST)

    def first_own(chip_to):
        return pltpu.make_async_remote_copy(
            src_ref=sel.at[chip_to, pl.ds(1, 2)],
            dst_ref=pad_own.at[chip],
            send_sem=s1, recv_sem=r1_own,
            device_id=(ctx_of(chip_to, core), y), device_id_type=MESH,
        )

    def first_other(chip_to):
        return pltpu.make_async_remote_copy(
            src_ref=sel.at[chip_to, 0],
            dst_ref=pad_other.at[chip],
            send_sem=s1, recv_sem=r1_other,
            device_id=(ctx_of(chip_to, 1 - core), y), device_id_type=MESH,
        )

    trips = [(dz, dx) for dz in range(2) for dx in range(4)][1:]
    for dz, dx in sorted(trips, key=lambda t: -(t[0] + min(t[1], 4 - t[1]))):
        chip_to = (half + dz) % 2 * 4 + (x + dx) % 4
        first_own(chip_to).start()
        first_other(chip_to).start()
    first_other(chip).start()
    pad_own[chip] = sel[chip, 1:3]

    def weights(step):
        y_to = (y + step) % 4
        return pltpu.make_async_remote_copy(
            src_ref=w_hbm.at[
                pl.ds(pl.multiple_of(core * half_rows, half_rows), half_rows),
                pl.ds(pl.multiple_of(y_to * w_cols, w_cols), w_cols),
            ],
            dst_ref=wbuf.at[
                pl.ds(pl.multiple_of(y * w_rows + core * half_rows, half_rows), half_rows), :
            ],
            send_sem=s_w, recv_sem=r_w.at[step - 1],
            device_id=(ctx, y_to), device_id_type=MESH,
        )

    for step in (1, 3, 2):
        weights(step).start()

    row = chosen_ref[pl.ds(block, 1), :]
    diagonal = lax.broadcasted_iota(jnp.int32, (PICK, PICK), 0) == lax.broadcasted_iota(
        jnp.int32, (PICK, PICK), 1
    )
    column = jnp.sum(jnp.where(diagonal, row, 0), axis=1, keepdims=True)

    def base_of(device):
        return block * 2048 + (half * 15 + (1 - 2 * half) * device) * PIECE

    slot = lax.broadcasted_iota(jnp.int32, (1, GROUP * MOST), 1)
    slot_core = (core + slot // (CHIPS * MOST)) % 2
    base = base_of(slot // MOST % CHIPS * 2 + slot_core)
    first = jnp.sum((column < base).astype(jnp.int32), axis=0, keepdims=True)
    inside = (column >= base) & (column < base + PIECE)
    entry = lax.broadcasted_iota(jnp.int32, (PICK, GROUP * MOST), 0)
    pick[...] = ((entry - first == slot % MOST) & inside).astype(F32).astype(BF16)
    q_place = (first + slot % MOST)[:, : CHIPS * MOST]

    arrived = pad_own.at[pl.ds(0, CHIPS - 1)]
    pltpu.make_async_copy(arrived, arrived, r1_own).wait()
    pltpu.make_async_copy(pad_other, pad_other, r1_other).wait()

    def rows_of(kind, z_from):
        return pl.ds(pl.multiple_of((kind * RING + z_from) * PICK, PICK), PICK)

    own_side = jnp.dot(
        pick[:, : CHIPS * MOST],
        pad_own[:, 0].reshape(CHIPS * MOST, HD),
        preferred_element_type=F32,
    )
    other_side = jnp.dot(
        pick[:, CHIPS * MOST :],
        pad_other[...].reshape(CHIPS * MOST, HD),
        preferred_element_type=F32,
    )
    block_rows = own_side + other_side
    top_rows, low_rows = block_rows[:HD], block_rows[HD:]

    @pl.when(core == 0)
    def _():
        kv[rows_of(core, z), :] = block_rows.astype(BF16)

    @pl.when(core == 1)
    def _():
        kv[rows_of(core, z), :] = jnp.concatenate([top_rows.T, low_rows.T], axis=0).astype(BF16)


    ways = ((0, 1), (1, -1))
    sent_rows = []

    def rows_of_sub(z_from, sub):
        return pl.ds(pl.multiple_of((core * RING + z_from) * PICK + sub * SUB, SUB), SUB)

    def arrival(side, offset, sub):
        return r2.at[(side * 8 + offset - 1) * SUBS + sub]

    def send(pred, z_from, sub, delta, side, offset):
        rows = rows_of_sub(z_from, sub)
        copy = pltpu.make_async_remote_copy(
            src_ref=kv.at[rows, :], dst_ref=kv.at[rows, :],
            send_sem=s2.at[len(sent_rows)], recv_sem=arrival(side, offset, sub),
            device_id=(ctx_at(at(delta), core), y), device_id_type=MESH,
        )
        sent_rows.append((pred, copy))

        @pl.when(pred)
        def _():
            copy.start()

    def comes(stops, z_from, side, offset, sub):
        if offset == 8 and side != sub * 2 // SUBS:
            return False
        is_wanted = needs((z_from + RING + ways[side][1] * offset) % RING, z_from)
        for stop, before in stops.items():
            if before == offset:
                further = comes(stops, z_from, side, stop, sub)
                if further is not False:
                    is_wanted = is_wanted | further
        return is_wanted

    def send_on(is_mine, stops, z_from, offset, side, sub):
        for stop, before in stops.items():
            if before == offset:
                goes = comes(stops, z_from, side, stop, sub)
                if goes is not False:
                    send(is_mine & goes, z_from, sub, ways[side][1] * (stop - offset), side, stop)

    def receive(offset):
        cases = [(half == 1, EARLY)] if offset % 2 else [(half == 0, EARLY), (half == 1, LATE)]
        for sub in range(SUBS):
            for side, way in ways:
                z_from = at(-way * offset)
                came = False
                for is_mine, stops in cases:
                    here = comes(stops, z_from, side, offset, sub)
                    if here is not False:
                        came = (is_mine & here) if came is False else came | (is_mine & here)
                if came is False:
                    continue

                @pl.when(came)
                def _():
                    rows = rows_of_sub(z_from, sub)
                    pltpu.make_async_copy(
                        kv.at[rows, :], kv.at[rows, :], arrival(side, offset, sub)
                    ).wait()

                for is_mine, stops in cases:
                    send_on(is_mine, stops, z_from, offset, side, sub)
        for z_from in (at(-offset), at(offset))[: 1 if offset == 8 else 2]:

            @pl.when(needs(z, z_from))
            def _():
                to_sibling(z_from).start()

    def to_sibling(z_from):
        rows = rows_of(core, z_from)
        return pltpu.make_async_remote_copy(
            src_ref=kv.at[rows, :], dst_ref=kv.at[rows, :],
            send_sem=s_sib.at[z_from], recv_sem=r_sib.at[z_from],
            device_id=(sibling, y), device_id_type=MESH,
        )

    for sub in range(SUBS):
        for side, way in ways:
            send_on(half == 0, EARLY, z, 0, side, sub)
            send_on(half == 1, LATE, z, 0, side, sub)
    to_sibling(z).start()

    scale = HD**-0.5 * 1.4426950408889634

    def from_sibling(z_from):
        rows = rows_of(1 - core, z_from)
        pltpu.make_async_copy(kv.at[rows, :], kv.at[rows, :], r_sib.at[z_from]).wait()

    queries = pad_own.at[:, 1]

    def scores_of(z_from):
        return dot_nt(kv[rows_of(0, z_from), :], queries[...].reshape(CHIPS * MOST, HD)) * scale

    def summed(weight, z_from):
        values = kv[rows_of(1, z_from), :]
        weight = weight.astype(BF16)
        return jnp.dot(values[:HD], weight[:HD], preferred_element_type=F32) + jnp.dot(
            values[HD:], weight[HD:], preferred_element_type=F32
        )

    def attend_own():
        from_sibling(z)
        seen = lax.broadcasted_iota(jnp.int32, (PICK, PICK), 0) <= q_place
        scores = jnp.where(seen, scores_of(z), -1e30)
        top_now = jnp.max(scores, axis=0, keepdims=True)
        weight = jnp.exp2(scores - top_now)
        top[...] = top_now
        total[...] = jnp.sum(weight, axis=0, keepdims=True)
        acc[...] = summed(weight, z)

    def attend_these(z_froms):
        scores = [scores_of(z_from) for z_from in z_froms]
        top_was = top[...]
        top_now = top_was
        for part in scores:
            top_now = jnp.maximum(top_now, jnp.max(part, axis=0, keepdims=True))
        fade = jnp.exp2(top_was - top_now)
        total_now = total[...] * fade
        acc_now = acc[...] * fade
        for part, z_from in zip(scores, z_froms):
            weight = jnp.exp2(part - top_now)
            total_now += jnp.sum(weight, axis=0, keepdims=True)
            acc_now += summed(weight, z_from)
        top[...] = top_now
        total[...] = total_now
        acc[...] = acc_now

    def attend(z_from):
        @pl.when(needs(z, z_from))
        def _():
            from_sibling(z_from)
            attend_these([z_from])

    def attend_both(offset):
        left, right = at(-offset), at(offset)
        wants_left, wants_right = needs(z, left), needs(z, right)

        @pl.when(wants_left)
        def _():
            from_sibling(left)

        @pl.when(wants_right)
        def _():
            from_sibling(right)

        @pl.when(wants_left & wants_right)
        def _():
            attend_these([left, right])

        @pl.when(wants_left != wants_right)
        def _():
            attend_these([lax.select(wants_left, left, right)])

    for step in ORDER:
        if step == "own":
            attend_own()
        elif step < 0:
            receive(-step)
        elif step == 8:
            attend(at(8))
        else:
            attend_both(step)

    osend[...] = (acc[...] / total[...]).T.astype(BF16)

    att_rows = pl.ds(pl.multiple_of(half * MOST, MOST), MOST)
    att_cols = pl.ds(pl.multiple_of((y * 4 + x) * HD, HD), HD)

    def back(chip_to, y_to):
        return pltpu.make_async_remote_copy(
            src_ref=osend.at[pl.ds(pl.multiple_of(chip_to * MOST, MOST), MOST), :],
            dst_ref=att.at[att_rows, att_cols],
            send_sem=s3, recv_sem=r3,
            device_id=(ctx_of(chip_to, core), y_to), device_id_type=MESH,
        )

    def steps(there):
        return min(there, 4 - there)

    trips = [(dz, dx, dy) for dz in range(2) for dx in range(4) for dy in range(4)][1:]
    for dz, dx, dy in sorted(trips, key=lambda t: -(t[0] + steps(t[1]) + steps(t[2]))):
        back((half + dz) % 2 * 4 + (x + dx) % 4, (y + dy) % 4).start()
    att[att_rows, att_cols] = osend[my_q_rows, :]

    def pass_on(step):
        y_from = (y + 4 - step) % 4
        rows = pl.ds(pl.multiple_of(y_from * w_rows + core * half_rows, half_rows), half_rows)
        pltpu.make_async_copy(wbuf.at[rows, :], wbuf.at[rows, :], r_w.at[step - 1]).wait()
        pltpu.make_async_remote_copy(
            src_ref=wbuf.at[rows, :], dst_ref=wbuf.at[rows, :],
            send_sem=s_wf, recv_sem=r_wf,
            device_id=(sibling, y), device_id_type=MESH,
        ).start()

    for step in (1, 3, 2):
        pass_on(step)
    own_w.wait()
    three = wbuf.at[pl.ds(0, 3 * half_rows), :]
    pltpu.make_async_copy(three, three, r_wf).wait()
    pltpu.make_async_copy(kv.at[pl.ds(0, 31 * MOST), :], kv.at[pl.ds(0, 31 * MOST), :], r3).wait()

    updates = jnp.dot(att[...], wbuf[...], preferred_element_type=F32) * rsel[...]
    updates = updates.astype(BF16)
    for hf in range(2):
        out_ref[hf * PIECE : (hf + 1) * PIECE, :] = jnp.dot(
            place[hf], updates[hf * MOST : (hf + 1) * MOST, :], preferred_element_type=F32
        ).astype(BF16)

    pltpu.make_async_copy(arrived, arrived, s1).wait()
    pltpu.make_async_copy(pad_other, pad_other, s1).wait()
    for pred, copy in sent_rows:

        @pl.when(pred)
        def _():
            copy.wait_send()

    def sibling_sent(z_from, carry):
        @pl.when(needs(z, z_from) | (z_from == z))
        def _():
            to_sibling(z_from).wait_send()

        return carry

    lax.fori_loop(0, RING, sibling_sent, 0)
    sent = kv.at[pl.ds(0, 31 * MOST), :]
    pltpu.make_async_copy(sent, sent, s3).wait()
    pltpu.make_async_copy(three, three, s_w).wait()
    pltpu.make_async_copy(three, three, s_wf).wait()


def shards(queries, key_proj, value_proj, router, chosen, out_weight):
    tok_rows = queries.shape[0]
    w_cols = out_weight.shape[1] // 4
    dma = pltpu.SemaphoreType.DMA
    vmem = pl.BlockSpec(memory_space=pltpu.VMEM)
    hbm = pl.BlockSpec(memory_space=pltpu.HBM)
    return pl.pallas_call(
        body,
        out_shape=jax.ShapeDtypeStruct((tok_rows, w_cols), BF16),
        in_specs=[hbm] * 6,
        out_specs=vmem,
        scratch_shapes=[
            pltpu.VMEM(queries.shape, BF16),
            pltpu.VMEM(key_proj.shape, BF16),
            pltpu.VMEM(value_proj.shape, BF16),
            pltpu.VMEM(router.shape, BF16),
            pltpu.VMEM(chosen.shape, jnp.int32),
            dma((5,)),
            pltpu.VMEM((CHIPS, 3, MOST, HD), BF16),
            pltpu.VMEM((CHIPS, 2, MOST, HD), BF16),
            pltpu.VMEM((CHIPS, MOST, HD), BF16),
            pltpu.VMEM((2 * RING * PICK, HD), BF16),
            pltpu.VMEM((2 * MOST, 16 * HD), BF16),
            pltpu.VMEM((CHIPS * MOST, HD), BF16),
            pltpu.VMEM((4 * out_weight.shape[0], w_cols), BF16),
            pltpu.VMEM((2, PIECE, MOST), BF16),
            pltpu.VMEM((2 * MOST, 1), F32),
            pltpu.VMEM((1, CHIPS * MOST), F32),
            pltpu.VMEM((1, CHIPS * MOST), F32),
            pltpu.VMEM((HD, CHIPS * MOST), F32),
            pltpu.VMEM((PICK, GROUP * MOST), BF16),
            dma, dma, dma,
            dma((64,)), dma((16 * SUBS,)),
            dma((RING,)), dma((RING,)),
            dma, dma,
            dma, dma((3,)), dma, dma, dma,
        ],
        compiler_params=pltpu.CompilerParams(
            collective_id=0, has_side_effects=True, vmem_limit_bytes=60 * 1024 * 1024
        ),
        name="routed_attention",
    )(queries, key_proj, value_proj, router, chosen, out_weight)


def solution(mesh):
    placed = (P("ctx", "tp"), P("ctx", "tp"), P("ctx", "tp"), P("ctx"), P(), P("tp", None))
    return jax.shard_map(
        shards, mesh=mesh, in_specs=placed, out_specs=P("ctx", "tp"), check_vma=False
    )
```

time: 52.9 us -> 50.7 us (0.958)
  local copies, waits for them, and re-layouts: 3.09 us -> 1.87 us
  Pallas kernels: 49.3 us -> 48.7 us
    reshape x1 -> x0, local copies, waits for them, and re-layouts: 1.22 us -> none  [shards(): router.reshape(1, tok_rows)]
    pallas_call x1, Pallas kernels: 49.3 us -> 48.7 us  [shards(): pl.pallas_call(body, out_shape=jax.ShapeDtypeStruct((tok_rows, w_cols), B...]
where the time goes in v3:
time: 50.7 us; the launch traced here: 50.5 us
  Pallas kernels  48.7 us (96%)
  local copies, waits for them, and re-layouts  1.87 us (4%)
    pallas_call x1, Pallas kernels, shards(): pl.pallas_call(body, out_shape=jax.ShapeDtypeStruct((tok_rows, w_cols), B...  48.7 us
    unnamed x1, local copies, waits for them, and re-layouts  1.87 us

profile of v3, /device:TPU:1, one launch (start us, length us, event | category | flops | bytes accessed | tf_op | source)
XLA Modules:
  0.0 50.5 jit_solution(1292137679029008707)
XLA Ops:
  0.0 48.7 %routed_attention.1 = bf16[256,1024]{1,0:T(8,128)(2,1)} custom-call(bf16[256,512]{1,0:T(8,128)(2,1)} %q_hbm.1, bf16[256,512]{1,0:T(8,128)(2,1)} %k_hbm.1, bf16[256,512]{1,0:T(8,128)(2,1)} %v_hbm.1, bf16[256]{0:T(256)(128)(2,1)} %router_hbm.1, s32[16,256]{1,0:T(8,128)} %chosen_hbm.1, bf16[512,4096]{1,0:T(8,128)(2,1)} %w_hbm.1), custom_call_target="tpu_custom_call" | custom-call | tf_op jit(solution)/shard_map/routed_attention/pallas_call | solution.py:480
  48.7 1.9 %copy.8 = bf16[256,1024]{1,0:T(8,128)(2,1)} copy(bf16[256,1024]{1,0:T(8,128)(2,1)} %routed_attention.1) | data formatting | bytes 1048576

commit v4 on v3

--- a/solution.py
+++ b/solution.py
@@ -17,7 +17,7 @@
 SUB = PICK // SUBS
 EARLY = {1: 0, 3: 1, 2: 1, 5: 3, 4: 3, 7: 5, 6: 5, 8: 7}
 LATE = {2: 0, 4: 2, 6: 4, 8: 6}
-ORDER = (-1, -2, "own", -3, -4, 1, 2, -5, -6, 3, 4, -7, -8, 5, 6, 7, 8)
+ORDER = (-1, -2, "own", -3, -4, 1, 2, -5, -6, "share", 3, 4, -7, -8, 5, 6, 7, 8)
 MESH = pl.DeviceIdType.MESH
 F32 = jnp.float32
 BF16 = jnp.bfloat16
@@ -50,8 +50,8 @@
 
 def body(
     q_hbm, k_hbm, v_hbm, router_hbm, chosen_hbm, w_hbm, out_ref,
-    q_ref, k_ref, v_ref, router_ref, chosen_ref, l_in, sel, pad_own, pad_other, kv, att, osend, wbuf, place, rsel, top, total, acc, pick,
-    s1, r1_own, r1_other, s2, r2, s_sib, r_sib, s3, r3, s_w, r_w, s_wf, r_wf, l_w,
+    q_ref, k_ref, v_ref, router_ref, chosen_ref, l_in, sel, pad_own, pad_other, pad_query, kv, att, osend, wbuf, place, rsel, top, total, acc, pick,
+    s1, r1_own, r1_other, r1_query, s2, r2, s_sib, r_sib, s3, r3, s_w, r_w, s_wf, r_wf, l_w,
 ):
     ctx = lax.axis_index("ctx")
     y = lax.axis_index("tp")
@@ -130,24 +130,28 @@
     )
     own_w.start()
 
-    for load in loads:
+    for load in loads[:3]:
         load.wait()
+
+    picks_of = []
+    ones = []
+
+    def select(hf, kind, ref):
+        picked = jnp.dot(
+            picks_of[hf], ref[hf * PIECE : (hf + 1) * PIECE, :], preferred_element_type=F32
+        ).astype(BF16)
+        for head in range(4):
+            sel[hf * 4 + head, kind] = picked[:, head * HD : (head + 1) * HD]
 
     for hf in range(2):
         piece = ctx if hf == 0 else 255 - ctx
         row = chosen_ref[pl.ds(piece // GROUP, 1), :]
         by_rank, by_token = one_hots(row, piece * PIECE)
         picks = dot_nt(by_rank, by_token)
-        pick_bf = picks.astype(BF16)
-        place[hf] = dot_nt(by_token, by_rank).astype(BF16)
-        rows = slice(hf * PIECE, (hf + 1) * PIECE)
-        rsel[hf * MOST : (hf + 1) * MOST, :] = jnp.sum(
-            picks * router_ref[rows].astype(F32).reshape(1, PIECE), axis=1, keepdims=True
-        )
-        for kind, ref in ((1 - core, k_ref), (core, v_ref), (2, q_ref)):
-            picked = jnp.dot(pick_bf, ref[rows, :], preferred_element_type=F32).astype(BF16)
-            for head in range(4):
-                sel[hf * 4 + head, kind] = picked[:, head * HD : (head + 1) * HD]
+        ones.append((by_rank, by_token, picks))
+        picks_of.append(picks.astype(BF16))
+        for kind, ref in ((1 - core, k_ref), (core, v_ref)):
+            select(hf, kind, ref)
 
     pl.semaphore_wait(barrier, 18 + len(even_far) + (len(odd_far) - len(even_far)) * half)
 
@@ -155,9 +159,17 @@
 
     def first_own(chip_to):
         return pltpu.make_async_remote_copy(
-            src_ref=sel.at[chip_to, pl.ds(1, 2)],
+            src_ref=sel.at[chip_to, 1],
             dst_ref=pad_own.at[chip],
             send_sem=s1, recv_sem=r1_own,
+            device_id=(ctx_of(chip_to, core), y), device_id_type=MESH,
+        )
+
+    def first_query(chip_to):
+        return pltpu.make_async_remote_copy(
+            src_ref=sel.at[chip_to, 2],
+            dst_ref=pad_query.at[chip],
+            send_sem=s1, recv_sem=r1_query,
             device_id=(ctx_of(chip_to, core), y), device_id_type=MESH,
         )
 
@@ -175,23 +187,60 @@
         first_own(chip_to).start()
         first_other(chip_to).start()
     first_other(chip).start()
-    pad_own[chip] = sel[chip, 1:3]
+    pad_own[chip] = sel[chip, 1]
+    loads[3].wait()
+    for hf in range(2):
+        select(hf, 2, q_ref)
+    for dz, dx in trips:
+        first_query((half + dz) % 2 * 4 + (x + dx) % 4).start()
+    pad_query[chip] = sel[chip, 2]
+    loads[4].wait()
+    for hf, (by_rank, by_token, picks) in enumerate(ones):
+        place[hf] = dot_nt(by_token, by_rank).astype(BF16)
+        rows = slice(hf * PIECE, (hf + 1) * PIECE)
+        rsel[hf * MOST : (hf + 1) * MOST, :] = jnp.sum(
+            picks * router_ref[rows].astype(F32).reshape(1, PIECE), axis=1, keepdims=True
+        )
+
+    quarter_rows = w_rows // 4
+    beside = ctx + 2 - x % 2 * 4
+
+    def weight_rows(y_from, step, x_of):
+        if step == 2:
+            first_row = y_from * w_rows + (x_of % 2 * 2 + core) * quarter_rows
+            return pl.ds(pl.multiple_of(first_row, quarter_rows), quarter_rows)
+        return pl.ds(pl.multiple_of(y_from * w_rows + core * half_rows, half_rows), half_rows)
 
     def weights(step):
         y_to = (y + step) % 4
         return pltpu.make_async_remote_copy(
             src_ref=w_hbm.at[
-                pl.ds(pl.multiple_of(core * half_rows, half_rows), half_rows),
-                pl.ds(pl.multiple_of(y_to * w_cols, w_cols), w_cols),
+                weight_rows(0, step, x), pl.ds(pl.multiple_of(y_to * w_cols, w_cols), w_cols)
             ],
-            dst_ref=wbuf.at[
-                pl.ds(pl.multiple_of(y * w_rows + core * half_rows, half_rows), half_rows), :
-            ],
+            dst_ref=wbuf.at[weight_rows(y, step, x), :],
             send_sem=s_w, recv_sem=r_w.at[step - 1],
             device_id=(ctx, y_to), device_id_type=MESH,
         )
 
-    for step in (1, 3, 2):
+    def pass_on(rows, arrived_by, to, lands_by):
+        pltpu.make_async_copy(wbuf.at[rows, :], wbuf.at[rows, :], arrived_by).wait()
+        for ctx_to, sem in zip(to, lands_by):
+            pltpu.make_async_remote_copy(
+                src_ref=wbuf.at[rows, :], dst_ref=wbuf.at[rows, :],
+                send_sem=s_wf, recv_sem=sem,
+                device_id=(ctx_to, y), device_id_type=MESH,
+            ).start()
+
+    def share_weights():
+        rows = weight_rows((y + 2) % 4, 2, x)
+        pass_on(rows, r_w.at[1], (beside, sibling), (r_w.at[3], r_wf))
+
+    def finish_weights():
+        pass_on(weight_rows((y + 3) % 4, 1, x), r_w.at[0], (sibling,), (r_wf,))
+        pass_on(weight_rows((y + 1) % 4, 3, x), r_w.at[2], (sibling,), (r_wf,))
+        pass_on(weight_rows((y + 2) % 4, 2, x + 1), r_w.at[3], (sibling,), (r_wf,))
+
+    for step in (2, 1, 3):
         weights(step).start()
 
     row = chosen_ref[pl.ds(block, 1), :]
@@ -221,7 +270,7 @@
 
     own_side = jnp.dot(
         pick[:, : CHIPS * MOST],
-        pad_own[:, 0].reshape(CHIPS * MOST, HD),
+        pad_own[...].reshape(CHIPS * MOST, HD),
         preferred_element_type=F32,
     )
     other_side = jnp.dot(
@@ -323,16 +372,17 @@
             send_on(half == 1, LATE, z, 0, side, sub)
     to_sibling(z).start()
 
+    pltpu.make_async_copy(arrived, arrived, r1_query).wait()
+
     scale = HD**-0.5 * 1.4426950408889634
 
     def from_sibling(z_from):
         rows = rows_of(1 - core, z_from)
         pltpu.make_async_copy(kv.at[rows, :], kv.at[rows, :], r_sib.at[z_from]).wait()
 
-    queries = pad_own.at[:, 1]
 
     def scores_of(z_from):
-        return dot_nt(kv[rows_of(0, z_from), :], queries[...].reshape(CHIPS * MOST, HD)) * scale
+        return dot_nt(kv[rows_of(0, z_from), :], pad_query[...].reshape(CHIPS * MOST, HD)) * scale
 
     def summed(weight, z_from):
         values = kv[rows_of(1, z_from), :]
@@ -397,6 +447,8 @@
     for step in ORDER:
         if step == "own":
             attend_own()
+        elif step == "share":
+            share_weights()
         elif step < 0:
             receive(-step)
         elif step == 8:
@@ -425,18 +477,7 @@
         back((half + dz) % 2 * 4 + (x + dx) % 4, (y + dy) % 4).start()
     att[att_rows, att_cols] = osend[my_q_rows, :]
 
-    def pass_on(step):
-        y_from = (y + 4 - step) % 4
-        rows = pl.ds(pl.multiple_of(y_from * w_rows + core * half_rows, half_rows), half_rows)
-        pltpu.make_async_copy(wbuf.at[rows, :], wbuf.at[rows, :], r_w.at[step - 1]).wait()
-        pltpu.make_async_remote_copy(
-            src_ref=wbuf.at[rows, :], dst_ref=wbuf.at[rows, :],
-            send_sem=s_wf, recv_sem=r_wf,
-            device_id=(sibling, y), device_id_type=MESH,
-        ).start()
-
-    for step in (1, 3, 2):
-        pass_on(step)
+    finish_weights()
     own_w.wait()
     three = wbuf.at[pl.ds(0, 3 * half_rows), :]
     pltpu.make_async_copy(three, three, r_wf).wait()
@@ -450,6 +491,7 @@
         ).astype(BF16)
 
     pltpu.make_async_copy(arrived, arrived, s1).wait()
+    pltpu.make_async_copy(arrived, arrived, s1).wait()
     pltpu.make_async_copy(pad_other, pad_other, s1).wait()
     for pred, copy in sent_rows:
 
@@ -467,8 +509,9 @@
     lax.fori_loop(0, RING, sibling_sent, 0)
     sent = kv.at[pl.ds(0, 31 * MOST), :]
     pltpu.make_async_copy(sent, sent, s3).wait()
-    pltpu.make_async_copy(three, three, s_w).wait()
-    pltpu.make_async_copy(three, three, s_wf).wait()
+    for rows, sem in ((5 * quarter_rows, s_w), (7 * quarter_rows, s_wf)):
+        sent = wbuf.at[pl.ds(0, rows), :]
+        pltpu.make_async_copy(sent, sent, sem).wait()
 
 
 def shards(queries, key_proj, value_proj, router, chosen, out_weight):
@@ -490,8 +533,7 @@
             pltpu.VMEM(chosen.shape, jnp.int32),
             dma((5,)),
             pltpu.VMEM((CHIPS, 3, MOST, HD), BF16),
-            pltpu.VMEM((CHIPS, 2, MOST, HD), BF16),
-            pltpu.VMEM((CHIPS, MOST, HD), BF16),
+            *[pltpu.VMEM((CHIPS, MOST, HD), BF16)] * 3,
             pltpu.VMEM((2 * RING * PICK, HD), BF16),
             pltpu.VMEM((2 * MOST, 16 * HD), BF16),
             pltpu.VMEM((CHIPS * MOST, HD), BF16),
@@ -502,11 +544,11 @@
             pltpu.VMEM((1, CHIPS * MOST), F32),
             pltpu.VMEM((HD, CHIPS * MOST), F32),
             pltpu.VMEM((PICK, GROUP * MOST), BF16),
-            dma, dma, dma,
+            dma, dma, dma, dma,
             dma((64,)), dma((16 * SUBS,)),
             dma((RING,)), dma((RING,)),
             dma, dma,
-            dma, dma((3,)), dma, dma, dma,
+            dma, dma((4,)), dma, dma, dma,
         ],
         compiler_params=pltpu.CompilerParams(
             collective_id=0, has_side_effects=True, vmem_limit_bytes=60 * 1024 * 1024

time: 50.7 us -> 50.5 us (level)
  no operation moved by 1% of the time
where the time goes in v4:
time: 50.5 us; the launch traced here: 50.3 us
  Pallas kernels  48.4 us (96%)
  local copies, waits for them, and re-layouts  1.87 us (4%)
    pallas_call x1, Pallas kernels, shards(): pl.pallas_call(body, out_shape=jax.ShapeDtypeStruct((tok_rows, w_cols), B...  48.4 us
    unnamed x1, local copies, waits for them, and re-layouts  1.87 us

profile of v4, /device:TPU:1, one launch (start us, length us, event | category | flops | bytes accessed | tf_op | source)
XLA Modules:
  0.0 50.3 jit_solution(12452609285460557367)
XLA Ops:
  0.0 48.4 %routed_attention.1 = bf16[256,1024]{1,0:T(8,128)(2,1)} custom-call(bf16[256,512]{1,0:T(8,128)(2,1)} %q_hbm.1, bf16[256,512]{1,0:T(8,128)(2,1)} %k_hbm.1, bf16[256,512]{1,0:T(8,128)(2,1)} %v_hbm.1, bf16[256]{0:T(256)(128)(2,1)} %router_hbm.1, s32[16,256]{1,0:T(8,128)} %chosen_hbm.1, bf16[512,4096]{1,0:T(8,128)(2,1)} %w_hbm.1), custom_call_target="tpu_custom_call" | custom-call | tf_op jit(solution)/shard_map/routed_attention/pallas_call | solution.py:523
  48.5 1.9 %copy.8 = bf16[256,1024]{1,0:T(8,128)(2,1)} copy(bf16[256,1024]{1,0:T(8,128)(2,1)} %routed_attention.1) | data formatting | bytes 1048576

commit v5 on v4

--- a/solution.py
+++ b/solution.py
@@ -17,7 +17,7 @@
 SUB = PICK // SUBS
 EARLY = {1: 0, 3: 1, 2: 1, 5: 3, 4: 3, 7: 5, 6: 5, 8: 7}
 LATE = {2: 0, 4: 2, 6: 4, 8: 6}
-ORDER = (-1, -2, "own", -3, -4, 1, 2, -5, -6, "share", 3, 4, -7, -8, 5, 6, 7, 8)
+ORDER = (-1, -2, "own", -3, -4, 1, 2, -5, -6, "share", 3, 4, 5, 6, -7, -8, 7, 8)
 MESH = pl.DeviceIdType.MESH
 F32 = jnp.float32
 BF16 = jnp.bfloat16
@@ -352,14 +352,13 @@
 
                 for is_mine, stops in cases:
                     send_on(is_mine, stops, z_from, offset, side, sub)
-        for z_from in (at(-offset), at(offset))[: 1 if offset == 8 else 2]:
-
-            @pl.when(needs(z, z_from))
-            def _():
-                to_sibling(z_from).start()
-
-    def to_sibling(z_from):
-        rows = rows_of(core, z_from)
+
+                @pl.when(came & needs(z, z_from))
+                def _():
+                    to_sibling(z_from, rows_of_sub(z_from, sub)).start()
+
+    def to_sibling(z_from, rows=None):
+        rows = rows_of(core, z_from) if rows is None else rows
         return pltpu.make_async_remote_copy(
             src_ref=kv.at[rows, :], dst_ref=kv.at[rows, :],
             send_sem=s_sib.at[z_from], recv_sem=r_sib.at[z_from],

time: 50.5 us -> 50.7 us (level)
  no operation moved by 1% of the time
where the time goes in v5:
time: 50.7 us; the launch traced here: 50.5 us
  Pallas kernels  48.6 us (96%)
  local copies, waits for them, and re-layouts  1.87 us (4%)
    pallas_call x1, Pallas kernels, shards(): pl.pallas_call(body, out_shape=jax.ShapeDtypeStruct((tok_rows, w_cols), B...  48.6 us
    unnamed x1, local copies, waits for them, and re-layouts  1.87 us

profile of v5, /device:TPU:1, one launch (start us, length us, event | category | flops | bytes accessed | tf_op | source)
XLA Modules:
  0.0 50.5 jit_solution(9914597973118575633)
XLA Ops:
  0.0 48.6 %routed_attention.1 = bf16[256,1024]{1,0:T(8,128)(2,1)} custom-call(bf16[256,512]{1,0:T(8,128)(2,1)} %q_hbm.1, bf16[256,512]{1,0:T(8,128)(2,1)} %k_hbm.1, bf16[256,512]{1,0:T(8,128)(2,1)} %v_hbm.1, bf16[256]{0:T(256)(128)(2,1)} %router_hbm.1, s32[16,256]{1,0:T(8,128)} %chosen_hbm.1, bf16[512,4096]{1,0:T(8,128)(2,1)} %w_hbm.1), custom_call_target="tpu_custom_call" | custom-call | tf_op jit(solution)/shard_map/routed_attention/pallas_call | solution.py:522
  48.6 1.9 %copy.8 = bf16[256,1024]{1,0:T(8,128)(2,1)} copy(bf16[256,1024]{1,0:T(8,128)(2,1)} %routed_attention.1) | data formatting | bytes 1048576

commit v6 on v5

--- a/solution.py
+++ b/solution.py
@@ -17,7 +17,7 @@
 SUB = PICK // SUBS
 EARLY = {1: 0, 3: 1, 2: 1, 5: 3, 4: 3, 7: 5, 6: 5, 8: 7}
 LATE = {2: 0, 4: 2, 6: 4, 8: 6}
-ORDER = (-1, -2, "own", -3, -4, 1, 2, -5, -6, "share", 3, 4, 5, 6, -7, -8, 7, 8)
+ORDER = (-1, -2, "own", -3, -4, 1, 2, -5, -6, "share", 3, 4, -7, -8, 5, 6, 7, 8)
 MESH = pl.DeviceIdType.MESH
 F32 = jnp.float32
 BF16 = jnp.bfloat16

time: 50.7 us -> 50.5 us (level)
  no operation moved by 1% of the time
where the time goes in v6:
time: 50.5 us; the launch traced here: 50.3 us
  Pallas kernels  48.4 us (96%)
  local copies, waits for them, and re-layouts  1.87 us (4%)
    pallas_call x1, Pallas kernels, shards(): pl.pallas_call(body, out_shape=jax.ShapeDtypeStruct((tok_rows, w_cols), B...  48.4 us
    unnamed x1, local copies, waits for them, and re-layouts  1.87 us

profile of v6, /device:TPU:1, one launch (start us, length us, event | category | flops | bytes accessed | tf_op | source)
XLA Modules:
  0.0 50.3 jit_solution(13027106722858295180)
XLA Ops:
  0.0 48.4 %routed_attention.1 = bf16[256,1024]{1,0:T(8,128)(2,1)} custom-call(bf16[256,512]{1,0:T(8,128)(2,1)} %q_hbm.1, bf16[256,512]{1,0:T(8,128)(2,1)} %k_hbm.1, bf16[256,512]{1,0:T(8,128)(2,1)} %v_hbm.1, bf16[256]{0:T(256)(128)(2,1)} %router_hbm.1, s32[16,256]{1,0:T(8,128)} %chosen_hbm.1, bf16[512,4096]{1,0:T(8,128)(2,1)} %w_hbm.1), custom_call_target="tpu_custom_call" | custom-call | tf_op jit(solution)/shard_map/routed_attention/pallas_call | solution.py:522
  48.4 1.9 %copy.8 = bf16[256,1024]{1,0:T(8,128)(2,1)} copy(bf16[256,1024]{1,0:T(8,128)(2,1)} %routed_attention.1) | data formatting | bytes 1048576
